TPU v7x, 32 devices: a whole 2x2x4 slice. The times are simulated.
32 devices in a mesh: groups: 2 (over y), tensor: 4 (over x, core), task: 4 (over z).
Axes of the slice: x: 2, y: 2, z: 4, core: 2. Of those that a mesh axis runs over, the one named last changes fastest.
Arguments:
- tokens: bfloat16 [3072, 8192], P(('groups', 'task'), 'tensor'), parts along dimension 0, may hold values from -6 to 6
- task_counts: int32 [512], P(('groups', 'task')), parts along dimension 0, may hold values from 0 to 96, as said below
- task_embeddings: bfloat16 [512, 1024], P(('groups', 'task')), parts along dimension 0, may hold values from -6 to 6
- embedding_weight: bfloat16 [1024, 512], replicated, may hold values from -0.1875 to 0.1875
- down_factor_head: bfloat16 [512, 16, 8192], P('task', None, 'tensor'), may hold values from -0.0029296875 to 0.0029296875
- query_up_head: bfloat16 [512, 8, 4096], P('task', None, 'tensor'), may hold values from -0.09375 to 0.09375
- value_up_head: bfloat16 [512, 8, 1024], P('task', None, 'tensor'), may hold values from -0.09375 to 0.09375
- w_query: bfloat16 [8192, 4096], P('tensor'), may hold values from -0.0625 to 0.0625
- w_value: bfloat16 [8192, 1024], P('tensor'), may hold values from -0.0625 to 0.0625
Outputs:
- query: bfloat16 [3072, 4096], P(('groups', 'task', 'tensor')), parts along dimension 0
- value: bfloat16 [3072, 1024], P(('groups', 'task', 'tensor')), parts along dimension 0
- down_factors: bfloat16 [512, 16, 8192], P(('groups', 'task'), None, 'tensor'), parts along dimension 0
- query_up_factors: bfloat16 [512, 8, 4096], P(('groups', 'task'), None, 'tensor'), parts along dimension 0
- value_up_factors: bfloat16 [512, 8, 1024], P(('groups', 'task'), None, 'tensor'), parts along dimension 0
There are 2 independent parts, one for each index of `groups`. A program takes and returns all parts, laid end to end along the dimension named above; an argument that names none is the same for every part. Nothing has to cross between parts.
Inputs may be any that keep to these rules, and one draw needn't show every extreme that they name: For every k the task_counts of tasks k * 16 to k * 16 + 15 sum to at most 96; in every draw at least one task has exactly 96 tokens.
All inputs are finite; a program needn't handle non-finite values.
Results may differ from a plain program's by a relative error of at most 0.0059.
Values may be sent and summed in bfloat16 or wider, within the bound.
A program may use at most 128 MiB of HBM per device.

v0:
```python
import jax
import jax.numpy as jnp
from jax import lax
from jax.sharding import PartitionSpec as P

ADAPTER_SCALE = 2.0


def block_select(counts, groups, block_tasks, block_rows):
    tallies = counts.reshape(groups, block_tasks)
    finish = jnp.cumsum(tallies, axis=1)
    starts = finish - tallies
    positions = jnp.arange(block_rows, dtype=jnp.int32)
    inside = (positions[None, :, None] >= starts[:, None, :]) & (
        positions[None, :, None] < finish[:, None, :]
    )
    return inside.astype(jnp.float32)


def produce_head(hypernet_hidden, matrix):
    flattened = jnp.dot(
        hypernet_hidden, matrix.reshape(matrix.shape[0], -1), preferred_element_type=jnp.float32
    )
    return flattened.astype(jnp.bfloat16).reshape(
        hypernet_hidden.shape[0], matrix.shape[1], matrix.shape[2]
    )


def produce_adapters(
    task_embeddings, embedding_weight, down_factor_head, query_up_head, value_up_head
):
    hypernet_hidden = jax.nn.silu(
        jnp.dot(task_embeddings, embedding_weight, preferred_element_type=jnp.float32)
    ).astype(jnp.bfloat16)
    regrouped = (
        lax.all_to_all(down_factor_head, "task", split_axis=2, concat_axis=0, tiled=True),
        lax.all_to_all(query_up_head, "task", split_axis=2, concat_axis=0, tiled=True),
        lax.all_to_all(value_up_head, "task", split_axis=2, concat_axis=0, tiled=True),
    )
    every_hidden = lax.all_gather(hypernet_hidden, "task", axis=0, tiled=True)
    emitted_a = produce_head(every_hidden, regrouped[0])
    emitted_query = produce_head(every_hidden, regrouped[1])
    emitted_value = produce_head(every_hidden, regrouped[2])
    return (
        lax.all_to_all(emitted_a, "task", split_axis=0, concat_axis=2, tiled=True),
        lax.all_to_all(emitted_query, "task", split_axis=0, concat_axis=2, tiled=True),
        lax.all_to_all(emitted_value, "task", split_axis=0, concat_axis=2, tiled=True),
    )


def local(
    tokens,
    task_counts,
    task_embeddings,
    embedding_weight,
    down_factor_head,
    query_up_head,
    value_up_head,
    w_query,
    w_value,
):
    down_factors, query_up_factors, value_up_factors = produce_adapters(
        task_embeddings, embedding_weight, down_factor_head, query_up_head, value_up_head
    )
    parts_tensor = lax.axis_size("tensor")
    tok_rows, shard_width = tokens.shape
    block_rows = tok_rows // parts_tensor
    block_tasks = task_counts.shape[0] // parts_tensor
    adapter_rank_size = query_up_factors.shape[1]
    query_width = w_query.shape[1]
    collected_query, collected_value = (
        lax.all_gather(query_up_factors, "tensor", axis=2, tiled=True),
        lax.all_gather(value_up_factors, "tensor", axis=2, tiled=True),
    )
    count_of_blocks = block_rows * lax.axis_size("tensor") // block_rows
    base_product = jnp.concatenate(
        (
            jnp.dot(tokens, w_query, preferred_element_type=jnp.float32),
            jnp.dot(tokens, w_value, preferred_element_type=jnp.float32),
        ),
        axis=1,
    )
    task_adapters = down_factors.reshape(
        count_of_blocks, block_tasks, 2 * adapter_rank_size, shard_width
    )
    projected = jnp.einsum(
        "bpd,bmrd->bpmr",
        tokens.reshape(count_of_blocks, block_rows, shard_width),
        task_adapters,
        preferred_element_type=jnp.float32,
    )
    selected_factors = (
        projected * block_select(task_counts, count_of_blocks, block_tasks, block_rows)[..., None]
    )
    query_up_factor = collected_query.reshape(
        count_of_blocks, block_tasks, adapter_rank_size, -1
    ).astype(jnp.float32)
    value_up_factor = collected_value.reshape(
        count_of_blocks, block_tasks, adapter_rank_size, -1
    ).astype(jnp.float32)
    delta_query = jnp.einsum(
        "osxe,oxea->osa",
        selected_factors[..., :adapter_rank_size],
        query_up_factor,
        precision=lax.Precision.HIGHEST,
    )
    delta_value = jnp.einsum(
        "osxe,oxea->osa",
        selected_factors[..., adapter_rank_size:],
        value_up_factor,
        precision=lax.Precision.HIGHEST,
    )
    adapter_update = jnp.concatenate((delta_query, delta_value), axis=2).reshape(
        block_rows * lax.axis_size("tensor"), -1
    )
    combined_output = lax.psum_scatter(
        base_product + ADAPTER_SCALE * adapter_update, "tensor", scatter_dimension=0, tiled=True
    )
    return (
        combined_output[:, :query_width].astype(jnp.bfloat16),
        combined_output[:, query_width:].astype(jnp.bfloat16),
        down_factors,
        query_up_factors,
        value_up_factors,
    )


def solution(mesh):
    return jax.shard_map(
        local,
        mesh=mesh,
        in_specs=(
            P(("groups", "task"), "tensor"),
            P(("groups", "task")),
            P(("groups", "task"), None),
            P(),
            P("task", None, "tensor"),
            P("task", None, "tensor"),
            P("task", None, "tensor"),
            P("tensor", None),
            P("tensor", None),
        ),
        out_specs=(
            P(("groups", "task", "tensor"), None),
            P(("groups", "task", "tensor"), None),
            P(("groups", "task"), None, "tensor"),
            P(("groups", "task"), None, "tensor"),
            P(("groups", "task"), None, "tensor"),
        ),
        check_vma=False,
    )
```

profile of v0, /device:TPU:0, one launch (start us, length us, event | category | flops | bytes accessed | tf_op | source)
XLA Modules:
  0.0 591.4 jit_solution(5028770698183390571)
XLA Ops:
  7.2 0.0 copy-start
  7.2 0.0 copy-start.1
  7.2 4.6 copy.46
  11.8 6.4 %all-to-all-start.2 = ((bf16[128,8,1024]{0,1,2:T(8,128)(2,1)}), bf16[128,8,1024]{0,1,2:T(8,128)(2,1)}, u32[]{:S(2)}, u32[]{:S(2)}) async-start(bf16[128,8,1024]{0,1,2:T(8,128)(2,1)} %copy.46), calls=%async_computation.2 | async-start | bytes 4194304 | tf_op jit(solution)/shard_map/all_to_all | solution.py:37
  18.3 0.0 copy-done.1
  18.3 1.3 copy.49
  19.6 47.0 %all-to-all-done.2 = bf16[128,8,1024]{0,1,2:T(8,128)(2,1)} async-done(((bf16[128,8,1024]{0,1,2:T(8,128)(2,1)}), bf16[128,8,1024]{0,1,2:T(8,128)(2,1)}, u32[]{:S(2)}, u32[]{:S(2)}) %all-to-all-start.2) | async-done | bytes 2097184 | tf_op jit(solution)/shard_map/all_to_all | solution.py:37
  66.6 3.5 all-to-all-start.4
  70.1 0.0 copy-done.3
  70.1 1.6 multiply_convert_fusion
  71.6 20.0 %all_gather.9 = bf16[256,512]{1,0:T(8,128)(2,1)S(1)} all-gather(bf16[64,512]{1,0:T(8,128)(2,1)S(1)} %multiply_convert_fusion), channel_id=1, replica_groups=mesh['groups'=2,'tensor'=4,'task'=4] {'task'}, dimensions={0}, use_global_device_ids=true | all-gather | bytes 327680 | tf_op jit(solution)/shard_map/all_gather | solution.py:40
  91.7 4.8 copy.47
  96.5 2.3 copy.61
  98.8 0.7 convolution_convert_fusion.1
  99.5 1.3 copy.62
  100.8 0.0 all-to-all-done.4
  100.8 4.1 all-to-all-start.3
  104.9 13.4 %copy.43 = bf16[128,16,2048]{0,1,2:T(8,128)(2,1)} copy(bf16[128,16,2048]{2,1,0:T(8,128)(2,1)} %param.13) | data formatting | bytes 16777216 | tf_op args[4]
  118.2 8.9 %all-to-all-done.3 = bf16[256,8,256]{2,1,0:T(8,128)(2,1)S(1)} async-done(((bf16[256,8,256]{2,1,0:T(8,128)(2,1)}), bf16[256,8,256]{2,1,0:T(8,128)(2,1)S(1)}, u32[]{:S(2)}, u32[]{:S(2)}) %all-to-all-start.3) | async-done | bytes 1048608 | tf_op jit(solution)/shard_map/all_to_all | solution.py:46
  127.2 5.7 all-to-all-start
  132.9 0.0 all-gather.3.cloned.1.call-start
  132.9 1.1 copy.48
  134.0 0.0 all-gather.3.cloned.1.call-update
  134.0 0.4 copy.51
  134.5 0.3 convolution_convert_fusion.2
  134.8 0.1 copy.52
  134.9 0.3 copy.53
  135.3 1.1 reshape.80
  136.4 178.1 %all-to-all-done = bf16[128,16,2048]{0,1,2:T(8,128)(2,1)} async-done(((bf16[128,16,2048]{0,1,2:T(8,128)(2,1)}), bf16[128,16,2048]{0,1,2:T(8,128)(2,1)}, u32[]{:S(2)}, u32[]{:S(2)}) %all-to-all-start) | async-done | bytes 8388640 | tf_op jit(solution)/shard_map/all_to_all | solution.py:36
  314.4 3.4 all-to-all-start.5
  317.8 16.2 %copy.44 = bf16[128,16,4,512]{3,1,0,2:T(8,128)(2,1)} copy(bf16[128,16,4,512]{0,1,3,2:T(8,128)(2,1)} %bitcast) | data formatting | bytes 16777216 | tf_op jit(solution)/shard_map/all_to_all | solution.py:36
  334.0 16.4 %copy.59 = bf16[64,8,16,512]{3,1,2,0:T(8,128)(2,1)} copy(bf16[64,8,16,512]{3,2,1,0:T(8,128)(2,1)} %bitcast.74) | data formatting | bytes 16777216
  350.5 17.6 %convolution_convert_fusion = bf16[256,8192]{1,0:T(8,128)(2,1)S(1)} fusion(bf16[256,512]{1,0:T(8,128)(2,1)S(1)} %all_gather.9, bf16[512,8192]{1,0:T(8,128)(2,1)} %bitcast.76), kind=kOutput, calls=%fused_computation | convolution fusion | flops 2149580800 | bytes 12845056 | tf_op jit(solution)/shard_map/dot_general | solution.py:21
  368.0 3.9 copy.60
  371.9 0.0 all-to-all-done.5
  371.9 5.0 all-to-all-start.1
  376.9 0.0 all-gather.5.cloned.1.call-start
  376.9 0.3 reshape.81
  377.3 0.7 copy.71
  378.0 1.0 all_to_all.91
  379.0 0.0 all-gather.5.cloned.1.call-update
  379.1 0.0 copy-start.2
  379.1 0.0 reduce-scatter.2.cloned.1.call-start
  379.1 0.0 copy-done
  379.1 11.9 %fusion.7 = f32[384,4096]{1,0:T(8,128)} fusion(bf16[384,2048]{1,0:T(8,128)(2,1)S(1)} %copy-done, bf16[2048,4096]{1,0:T(8,128)(2,1)} %param.16), kind=kOutput, calls=%fused_computation.20 | convolution fusion | flops 6442450944 | bytes 24641536 | tf_op jit(solution)/shard_map/dot_general | solution.py:78
  391.0 0.0 copy-done.2
  391.0 0.1 reshape.70
  391.1 0.2 reduce_window_sum.11
  391.3 0.1 fusion.6
  391.4 4.0 fusion.8
  395.4 74.0 %all-to-all-done.1 = bf16[256,16,512]{2,1,0:T(8,128)(2,1)} async-done(((bf16[256,16,512]{2,1,0:T(8,128)(2,1)}), bf16[256,16,512]{2,1,0:T(8,128)(2,1)}, u32[]{:S(2)}, u32[]{:S(2)}) %all-to-all-start.1) | async-done | bytes 4194336 | tf_op jit(solution)/shard_map/all_to_all | solution.py:45
  469.4 12.5 %copy.70 = bf16[4,64,16,512]{3,0,2,1:T(4,128)(2,1)} copy(bf16[4,64,16,512]{3,2,1,0:T(8,128)(2,1)} %bitcast.2) | data formatting | bytes 8388608 | tf_op jit(solution)/shard_map/all_to_all | solution.py:45
  481.9 7.9 %reshape.68 = bf16[4,16,16,2048]{3,2,1,0:T(8,128)(2,1)} reshape(bf16[64,16,4,512]{3,2,1,0:T(4,128)(2,1)} %bitcast.72) | data formatting | bytes 8388608 | tf_op jit(solution)/shard_map/reshape | solution.py:83
  489.9 4.2 fusion
  494.1 7.6 %convolution_bitcast_fusion = f32[4,96,4096]{2,1,0:T(8,128)} fusion(bf16[4,16,8,4096]{3,2,1,0:T(8,128)(2,1)} %bitcast.85, f32[4,96,16,16]{1,3,2,0:T(8,128)} %fusion), kind=kOutput, calls=%fused_computation.3 | convolution fusion | flops 2415919104 | bytes 10747904 | tf_op jit(solution)/shard_map/osxe,oxea->osa/dot_general | solution.py:101
  501.6 2.1 convolution_bitcast_fusion.1
  503.8 3.7 maximum_multiply_fusion
  507.5 5.5 maximum_add_fusion
  513.0 0.0 reduce-scatter.2.cloned.1.call-update
  513.1 7.9 %all_to_all.92 = bf16[64,16,2048]{2,1,0:T(8,128)(2,1)} reshape(bf16[64,16,4,512]{3,2,1,0:T(4,128)(2,1)} %bitcast.73) | data formatting | bytes 8388608 | tf_op jit(solution)/shard_map/all_to_all | solution.py:45
  521.0 60.3 %reduce-scatter.2.cloned.1.call-done = f32[96,5120]{1,0:T(8,128)} async-done(((f32[384,5120]{1,0:T(8,128)}), f32[96,5120]{1,0:T(8,128)}) %reduce-scatter.2.cloned.1.call-update) | async-done | bytes 1966096 | tf_op jit(solution)/shard_map/reduce_scatter | solution.py:116
  581.3 1.7 convert.4
  583.0 0.9 slice.20
  583.9 0.7 slice.21
  (4 shorter events, 0.0 us)
Async XLA Ops:
  7.2 371.9 %copy-start = (bf16[384,2048]{1,0:T(8,128)(2,1)S(1)}, bf16[384,2048]{1,0:T(8,128)(2,1)}, u32[]{:S(2)}) copy-start(bf16[384,2048]{1,0:T(8,128)(2,1)} %param.9) | copy-start | bytes 4718596
  7.2 11.1 %copy-start.1 = (bf16[128,8,256]{2,1,0:T(8,128)(2,1)S(1)}, bf16[128,8,256]{2,1,0:T(8,128)(2,1)}, u32[]{:S(2)}) copy-start(bf16[128,8,256]{2,1,0:T(8,128)(2,1)} %param.15) | copy-start | bytes 1572868
  11.8 58.2 %copy-start.3 = (bf16[64,1024]{1,0:T(8,128)(2,1)S(1)}, bf16[64,1024]{1,0:T(8,128)(2,1)}, u32[]{:S(2)}) copy-start(bf16[64,1024]{1,0:T(8,128)(2,1)} %param.11) | copy-start | bytes 393220
  11.8 54.8 %all-to-all-start.2 = ((bf16[128,8,1024]{0,1,2:T(8,128)(2,1)}), bf16[128,8,1024]{0,1,2:T(8,128)(2,1)}, u32[]{:S(2)}, u32[]{:S(2)}) async-start(bf16[128,8,1024]{0,1,2:T(8,128)(2,1)} %copy.46), calls=%async_computation.2 | async-start | bytes 4194304 | tf_op jit(solution)/shard_map/all_to_all | solution.py:37
  66.6 34.2 %all-to-all-start.4 = ((bf16[128,8,256]{0,1,2:T(8,128)(2,1)}), bf16[128,8,256]{0,1,2:T(8,128)(2,1)S(1)}, u32[]{:S(2)}, u32[]{:S(2)}) async-start(bf16[128,8,256]{0,1,2:T(8,128)(2,1)} %copy.49), calls=%async_computation.4 | async-start | bytes 1048576 | tf_op jit(solution)/shard_map/all_to_all | solution.py:38
  100.8 26.4 %all-to-all-start.3 = ((bf16[256,8,256]{2,1,0:T(8,128)(2,1)}), bf16[256,8,256]{2,1,0:T(8,128)(2,1)S(1)}, u32[]{:S(2)}, u32[]{:S(2)}) async-start(bf16[256,8,256]{2,1,0:T(8,128)(2,1)} %bitcast.83), calls=%async_computation.3 | async-start | bytes 2097152 | tf_op jit(solution)/shard_map/all_to_all | solution.py:46
  127.2 187.2 %all-to-all-start = ((bf16[128,16,2048]{0,1,2:T(8,128)(2,1)}), bf16[128,16,2048]{0,1,2:T(8,128)(2,1)}, u32[]{:S(2)}, u32[]{:S(2)}) async-start(bf16[128,16,2048]{0,1,2:T(8,128)(2,1)} %copy.43), calls=%async_computation | async-start | bytes 16777216 | tf_op jit(solution)/shard_map/all_to_all | solution.py:36
  132.9 361.2 %all-gather.3.cloned.1.call-start = ((), (), s32[]{:S(2)}) async-start(), calls=%async_computation.7 | async-start | bytes 5242880 | tf_op jit(solution)/shard_map/all_gather | solution.py:72
  314.4 57.5 %all-to-all-start.5 = ((bf16[4,2,16384]{2,1,0:T(2,128)(2,1)}), bf16[4,2,16384]{2,1,0:T(2,128)(2,1)S(1)}, u32[]{:S(2)}, u32[]{:S(2)}) async-start(bf16[4,2,16384]{2,1,0:T(2,128)(2,1)} %reshape.80), calls=%async_computation.5 | async-start | bytes 524288 | tf_op jit(solution)/shard_map/all_to_all | solution.py:47
  371.9 97.5 %all-to-all-start.1 = ((bf16[256,16,512]{2,1,0:T(8,128)(2,1)}), bf16[256,16,512]{2,1,0:T(8,128)(2,1)}, u32[]{:S(2)}, u32[]{:S(2)}) async-start(bf16[256,16,512]{2,1,0:T(8,128)(2,1)} %bitcast.75), calls=%async_computation.1 | async-start | bytes 8388608 | tf_op jit(solution)/shard_map/all_to_all | solution.py:45
  376.9 124.7 %all-gather.5.cloned.1.call-start = ((), (), s32[]{:S(2)}) async-start(), calls=%async_computation.8 | async-start | bytes 1310720 | tf_op jit(solution)/shard_map/all_gather | solution.py:73
  379.1 12.0 %copy-start.2 = (s32[64]{0:T(128)S(1)}, s32[64]{0:T(128)}, u32[]{:S(2)}) copy-start(s32[64]{0:T(128)} %param.10) | copy-start | bytes 772
  379.1 202.3 %reduce-scatter.2.cloned.1.call-start = ((), (), s32[]{:S(2)}) async-start(), calls=%async_computation.9 | async-start | bytes 9830400 | tf_op jit(solution)/shard_map/reduce_scatter | solution.py:116
Sparse Core Ops, SparseCore 0:
  135.8 35.8 all-gather.2
  379.9 18.2 all-gather.4
  513.2 68.0 reduce-scatter.1
where the time goes:
time: 593 us; the launch traced here: 591 us
  waiting for transfers between devices  368 us (62%)
  local copies, waits for them, and re-layouts  99.4 us (17%)
  matrix products  50 us (8%)
  starting transfers between devices  28.2 us (5%)
  blocking collectives  20 us (3%)
  between operations  14.2 us (2%)
  other arithmetic  11.2 us (2%)
    all_to_all x1, waiting for transfers between devices, produce_adapters(): lax.all_to_all(down_factor_head, 'task', split_axis=2, concat_axis=0, til...  178 us
    all_to_all x1, waiting for transfers between devices, produce_adapters(): lax.all_to_all(emitted_a, 'task', split_axis=0, concat_axis=2, tiled=True)  74 us
    reduce_scatter x1, waiting for transfers between devices, local(): lax.psum_scatter(base_product + ADAPTER_SCALE * adapter_update, 'tensor',...  60.3 us
    all_to_all x1, waiting for transfers between devices, produce_adapters(): lax.all_to_all(query_up_head, 'task', split_axis=2, concat_axis=0, tiled=...  47 us
    unnamed x17, local copies, waits for them, and re-layouts  44.6 us
    all_to_all x2, local copies, waits for them, and re-layouts, produce_adapters(): lax.all_to_all(emitted_a, 'task', split_axis=0, concat_axis=2, tiled=True)  20.4 us
    all_gather x1, blocking collectives, produce_adapters(): every_hidden = lax.all_gather(hypernet_hidden, 'task', axis=0, tiled=True)  20 us
    dot_general x3, matrix products, produce_head(): jnp.dot(hypernet_hidden, matrix.reshape(matrix.shape[0], -1), preferred_e...  18.6 us
  transfers between devices with their start and end apart: 9, of which 5 were waited for; matrix products, arithmetic and copies ran while one was open for 22% of the time, Pallas kernels for 0%

commit v1 on v0

v1 whole, which is shorter than its diff:
```python
import jax
import jax.numpy as jnp
from jax import lax
from jax.sharding import PartitionSpec as P

ADAPTER_SCALE = 2.0


def block_member(counts, blocks, block_tasks, block_rows):
    tallies = counts.reshape(blocks, block_tasks)
    order = jnp.arange(block_tasks, dtype=jnp.int32)
    upto = order[None, :, None] >= order[None, None, :]
    finish = jnp.sum(jnp.where(upto, tallies[:, None, :], 0), axis=2)
    starts = finish - tallies
    positions = jnp.arange(block_rows, dtype=jnp.int32)
    inside = (positions[None, :, None] >= starts[:, None, :]) & (
        positions[None, :, None] < finish[:, None, :]
    )
    return inside.astype(jnp.float32)


def pack_head(head, n_groups, n_task):
    units, ranks, width = head.shape
    own = width // n_groups
    part = lax.dynamic_slice_in_dim(head, lax.axis_index("groups") * own, own, axis=2)
    part = part.reshape(units, ranks, n_task, own // n_task)
    return part.transpose(2, 0, 1, 3).reshape(n_task, units, -1)


def regroup(packed):
    got = lax.all_to_all(packed, "task", split_axis=0, concat_axis=0, tiled=True)
    return got.reshape(-1, got.shape[2])


def emit(every_hidden, matrix, n_owners):
    made = jnp.dot(every_hidden, matrix, preferred_element_type=jnp.float32)
    made = made.astype(jnp.bfloat16).reshape(n_owners, -1, matrix.shape[1])
    return lax.all_to_all(
        made, ("groups", "task"), split_axis=0, concat_axis=0, tiled=True
    )


def unpack_factor(got, ranks):
    owners, tasks, flat = got.shape
    return (
        got.reshape(owners, tasks, ranks, flat // ranks)
        .transpose(1, 2, 0, 3)
        .reshape(tasks, ranks, -1)
    )


def local(
    tokens,
    task_counts,
    task_embeddings,
    embedding_weight,
    down_factor_head,
    query_up_head,
    value_up_head,
    w_query,
    w_value,
):
    n_groups, n_task = lax.axis_size("groups"), lax.axis_size("task")
    n_owners = n_groups * n_task
    blocks = lax.axis_size("tensor")
    rank = query_up_head.shape[1]
    rows, shard_width = tokens.shape
    block_rows = rows // blocks
    block_tasks = task_counts.shape[0] // blocks

    low, high = down_factor_head[:, :rank], down_factor_head[:, rank:]
    down0 = regroup(pack_head(low, n_groups, n_task))
    down1 = regroup(pack_head(high, n_groups, n_task))
    packed_query = pack_head(query_up_head, n_groups, n_task)
    packed_value = pack_head(value_up_head, n_groups, n_task)
    up = regroup(jnp.concatenate((packed_query, packed_value), axis=2))

    hidden = jax.nn.silu(
        jnp.dot(task_embeddings, embedding_weight, preferred_element_type=jnp.float32)
    ).astype(jnp.bfloat16)
    every_hidden = lax.all_gather(hidden, ("groups", "task"), axis=0, tiled=True)

    base_query = lax.psum_scatter(
        jnp.dot(tokens, w_query, preferred_element_type=jnp.float32),
        "tensor", scatter_dimension=0, tiled=True,
    )
    base_value = lax.psum_scatter(
        jnp.dot(tokens, w_value, preferred_element_type=jnp.float32),
        "tensor", scatter_dimension=0, tiled=True,
    )

    half0 = unpack_factor(emit(every_hidden, down0, n_owners), rank)
    half1 = unpack_factor(emit(every_hidden, down1, n_owners), rank)
    got_up = emit(every_hidden, up, n_owners)
    flat_query = packed_query.shape[2]
    query_up_factors = unpack_factor(got_up[:, :, :flat_query], rank)
    value_up_factors = unpack_factor(got_up[:, :, flat_query:], rank)
    down_factors = jnp.concatenate((half0, half1), axis=1)

    member = block_member(task_counts, blocks, block_tasks, block_rows)
    stretches = tokens.reshape(blocks, block_rows, shard_width)

    def project(half):
        made = jnp.einsum(
            "bpd,bmrd->bpmr",
            stretches,
            half.reshape(blocks, block_tasks, rank, shard_width),
            preferred_element_type=jnp.float32,
        )
        return jnp.sum(made * member[..., None], axis=2).reshape(rows, rank)

    low_rank = lax.psum_scatter(
        jnp.concatenate((project(half0), project(half1)), axis=1),
        "tensor", scatter_dimension=0, tiled=True,
    )
    own_member = lax.dynamic_index_in_dim(
        member, lax.axis_index("tensor"), axis=0, keepdims=False
    )

    def delta(part, factors):
        spread = (own_member[:, :, None] * part[:, None, :]).reshape(block_rows, -1)
        whole = lax.all_to_all(factors, "tensor", split_axis=0, concat_axis=2, tiled=True)
        return jnp.dot(
            spread,
            whole.reshape(block_tasks * rank, -1).astype(jnp.float32),
            precision=lax.Precision.HIGHEST,
        )

    query = base_query + ADAPTER_SCALE * delta(low_rank[:, :rank], query_up_factors)
    value = base_value + ADAPTER_SCALE * delta(low_rank[:, rank:], value_up_factors)
    return (
        query.astype(jnp.bfloat16),
        value.astype(jnp.bfloat16),
        down_factors,
        query_up_factors,
        value_up_factors,
    )


def solution(mesh):
    return jax.shard_map(
        local,
        mesh=mesh,
        in_specs=(
            P(("groups", "task"), "tensor"),
            P(("groups", "task")),
            P(("groups", "task"), None),
            P(),
            P("task", None, "tensor"),
            P("task", None, "tensor"),
            P("task", None, "tensor"),
            P("tensor", None),
            P("tensor", None),
        ),
        out_specs=(
            P(("groups", "task", "tensor"), None),
            P(("groups", "task", "tensor"), None),
            P(("groups", "task"), None, "tensor"),
            P(("groups", "task"), None, "tensor"),
            P(("groups", "task"), None, "tensor"),
        ),
        check_vma=False,
    )
```

time: 593 us -> 431 us (0.73)
  waiting for transfers between devices: 368 us -> 126 us
  blocking collectives: 20 us -> 141 us
  local copies, waits for them, and re-layouts: 99.4 us -> 79.5 us
  matrix products: 50 us -> 38.3 us
  other arithmetic: 11.2 us -> 2.67 us
    all_to_all x6, waiting for transfers between devices: 308 us -> 126 us  [the longest x2 67.4 us: emit(): lax.all_to_all(made, ('groups', 'task'), split_axis=0, concat_axis=0, til...]
    all_to_all x0 -> x2, blocking collectives: none -> 67.8 us  [the longest x1 35.6 us: emit(): lax.all_to_all(made, ('groups', 'task'), split_axis=0, concat_axis=0, til...]
    reduce_scatter x1 -> x2, waiting for transfers between devices: 60.3 us -> 0.01 us  [the longest x1 0.01 us: local(): lax.psum_scatter(jnp.dot(tokens, w_value, preferred_element_type=jnp.floa...]
    all_gather x1, blocking collectives: 20 us -> 72.8 us  [local(): lax.all_gather(hidden, ('groups', 'task'), axis=0, tiled=True)]
    all_to_all x8 -> x4, local copies, waits for them, and re-layouts: 44.7 us -> 10.1 us  [the longest x2 8.08 us: regroup(): lax.all_to_all(packed, 'task', split_axis=0, concat_axis=0, tiled=True)]
    unnamed x17 -> x30, local copies, waits for them, and re-layouts: 44.6 us -> 22.4 us
    transpose x0 -> x7, local copies, waits for them, and re-layouts: none -> 17.1 us  [the longest x3 9.03 us: unpack_factor(): return got.reshape(owners, tasks, ranks, flat // ranks).transpose(1, 2, 0...]
    dot_general x7 -> x8, matrix products: 34.1 us -> 20.3 us  [the longest x3 9.23 us: emit(): made = jnp.dot(every_hidden, matrix, preferred_element_type=jnp.float32)]
  transfers between devices with their start and end apart: 9 -> 9, of which waited for: 5 -> 5; matrix products, arithmetic and copies ran while one was open for 22% -> 19% of each run, Pallas kernels for 0% -> 0%
where the time goes in v1:
time: 431 us; the launch traced here: 429 us
  blocking collectives  141 us (33%)
  waiting for transfers between devices  126 us (29%)
  local copies, waits for them, and re-layouts  79.5 us (18%)
  matrix products  38.3 us (9%)
  starting transfers between devices  27.9 us (6%)
  between operations  14 us (3%)
    all_gather x1, blocking collectives, local(): lax.all_gather(hidden, ('groups', 'task'), axis=0, tiled=True)  72.8 us
    all_to_all x2, waiting for transfers between devices, emit(): lax.all_to_all(made, ('groups', 'task'), split_axis=0, concat_axis=0, til...  67.4 us
    all_to_all x2, waiting for transfers between devices, regroup(): lax.all_to_all(packed, 'task', split_axis=0, concat_axis=0, tiled=True)  41 us
    all_to_all x1, blocking collectives, emit(): lax.all_to_all(made, ('groups', 'task'), split_axis=0, concat_axis=0, til...  35.6 us
    all_to_all x1, blocking collectives, regroup(): lax.all_to_all(packed, 'task', split_axis=0, concat_axis=0, tiled=True)  32.3 us
    unnamed x30, local copies, waits for them, and re-layouts  22.4 us
    all_to_all x2, waiting for transfers between devices, delta(): lax.all_to_all(factors, 'tensor', split_axis=0, concat_axis=2, tiled=True)  17.8 us
    dot_general x1, matrix products, local(): jnp.dot(tokens, w_query, preferred_element_type=jnp.float32)  12.4 us
  transfers between devices with their start and end apart: 9, of which 5 were waited for; matrix products, arithmetic and copies ran while one was open for 19% of the time, Pallas kernels for 0%

profile of v1, /device:TPU:0, one launch (start us, length us, event | category | flops | bytes accessed | tf_op | source)
XLA Modules:
  0.0 429.1 jit_solution(9203000711344419426)
XLA Ops:
  7.2 6.3 %fusion.18 = (bf16[128,8,2048]{2,1,0:T(8,128)(2,1)}, bf16[128,8,2048]{2,1,0:T(8,128)(2,1)}) fusion(bf16[128,16,2048]{2,1,0:T(8,128)(2,1)} %param.13), kind=kLoop, calls=%fused_computation.46 | loop fusion | bytes 16777216 | tf_op jit(solution)/shard_map/slice | solution.py:71
  13.5 4.6 %constant_dynamic-slice_fusion = (bf16[128,8,1024]{2,1,0:T(8,128)(2,1)}, bf16[128,8,1024]{2,1,0:T(8,128)(2,1)}) fusion(bf16[128,8,2048]{2,1,0:T(8,128)(2,1)} %get-tuple-element.46, s32[]{:T(128)S(6)} %select_n.20, bf16[128,8,2048]{2,1,0:T(8,128)(2,1)} %get-tuple-element.45), kind=kLoop, calls=%fused_computation.43 | loop fusion | bytes 8388612 | tf_op jit(solution)/shard_map/dynamic_slice | solution.py:25
  18.1 4.1 copy.174
  22.3 3.1 copy.148
  25.4 6.3 %all-to-all-start = ((bf16[4,128,2048]{1,2,0:T(8,128)(2,1)}), bf16[4,128,2048]{1,2,0:T(8,128)(2,1)}, u32[]{:S(2)}, u32[]{:S(2)}) async-start(bf16[4,128,2048]{1,2,0:T(8,128)(2,1)} %bitcast.137), calls=%async_computation.1 | async-start | bytes 4194304 | tf_op jit(solution)/shard_map/all_to_all | solution.py:31
  31.7 4.1 copy.176
  35.9 3.2 copy.153
  39.0 41.0 %all-to-all-done = bf16[4,128,2048]{1,2,0:T(8,128)(2,1)} async-done(((bf16[4,128,2048]{1,2,0:T(8,128)(2,1)}), bf16[4,128,2048]{1,2,0:T(8,128)(2,1)}, u32[]{:S(2)}, u32[]{:S(2)}) %all-to-all-start) | async-done | bytes 2097184 | tf_op jit(solution)/shard_map/all_to_all | solution.py:31
  80.0 4.6 %all-to-all-start.2 = ((bf16[4,128,2048]{1,2,0:T(8,128)(2,1)}), bf16[4,128,2048]{1,2,0:T(8,128)(2,1)}, u32[]{:S(2)}, u32[]{:S(2)}) async-start(bf16[4,128,2048]{1,2,0:T(8,128)(2,1)} %bitcast.136), calls=%async_computation.3 | async-start | bytes 4194304 | tf_op jit(solution)/shard_map/all_to_all | solution.py:31
  84.7 0.3 multiply_convert_fusion
  85.0 72.8 %all_gather.3 = bf16[512,512]{1,0:T(8,128)(2,1)S(1)} all-gather(bf16[64,512]{1,0:T(8,128)(2,1)S(1)} %multiply_convert_fusion), channel_id=1, replica_groups=mesh['groups'=2,'tensor'=4,'task'=4] {'groups','task'}, dimensions={0}, use_global_device_ids=true | all-gather | bytes 589824 | tf_op jit(solution)/shard_map/all_gather | solution.py:81
  157.8 4.1 copy.149
  161.9 4.2 convolution_convert_fusion.2
  166.1 4.3 %all-to-all-start.1 = ((bf16[8,64,2048]{2,1,0:T(8,128)(2,1)}), bf16[8,64,2048]{2,1,0:T(8,128)(2,1)}, u32[]{:S(2)}, u32[]{:S(2)}) async-start(bf16[8,64,2048]{2,1,0:T(8,128)(2,1)} %bitcast.150), calls=%async_computation.2 | async-start | bytes 4194304 | tf_op jit(solution)/shard_map/all_to_all | solution.py:38
  170.4 4.0 copy.154
  174.4 4.2 convolution_convert_fusion.1
  178.6 36.0 %all-to-all-done.1 = bf16[8,64,2048]{2,1,0:T(8,128)(2,1)} async-done(((bf16[8,64,2048]{2,1,0:T(8,128)(2,1)}), bf16[8,64,2048]{2,1,0:T(8,128)(2,1)}, u32[]{:S(2)}, u32[]{:S(2)}) %all-to-all-start.1) | async-done | bytes 2097184 | tf_op jit(solution)/shard_map/all_to_all | solution.py:38
  214.6 4.5 %all-to-all-start.3 = ((bf16[8,64,2048]{2,1,0:T(8,128)(2,1)}), bf16[8,64,2048]{2,1,0:T(8,128)(2,1)}, u32[]{:S(2)}, u32[]{:S(2)}) async-start(bf16[8,64,2048]{2,1,0:T(8,128)(2,1)} %bitcast.149), calls=%async_computation.4 | async-start | bytes 4194304 | tf_op jit(solution)/shard_map/all_to_all | solution.py:38
  219.1 0.2 reduce-scatter.10.cloned.1.call-start
  219.7 2.3 copy.183
  221.9 1.8 bitcast_bitcast_fusion.2
  223.7 3.6 copy.150
  227.3 4.2 reshape_reshape.6
  231.5 2.7 fusion.6
  234.3 31.4 %all-to-all-done.3 = bf16[8,64,2048]{2,1,0:T(8,128)(2,1)} async-done(((bf16[8,64,2048]{2,1,0:T(8,128)(2,1)}), bf16[8,64,2048]{2,1,0:T(8,128)(2,1)}, u32[]{:S(2)}, u32[]{:S(2)}) %all-to-all-start.3) | async-done | bytes 2097184 | tf_op jit(solution)/shard_map/all_to_all | solution.py:38
  265.7 2.3 copy.184
  268.0 1.7 bitcast_bitcast_fusion
  269.7 3.6 copy.155
  273.3 4.2 reshape_reshape.7
  277.6 2.7 fusion.7
  280.4 0.8 copy.171
  281.3 5.6 %fusion.21 = f32[384,1024]{1,0:T(8,128)} fusion(bf16[384,2048]{1,0:T(8,128)(2,1)} %param.9, bf16[2048,1024]{1,0:T(8,128)(2,1)} %param.17), kind=kOutput, calls=%fused_computation.49 | convolution fusion | flops 1610612736 | bytes 7340032 | tf_op jit(solution)/shard_map/dot_general | solution.py:88
  286.9 0.3 reduce-scatter.6.cloned.1.call-start
  287.2 12.4 %fusion.20 = f32[384,4096]{1,0:T(8,128)} fusion(bf16[384,2048]{1,0:T(8,128)(2,1)} %param.9, bf16[2048,4096]{1,0:T(8,128)(2,1)} %param.16), kind=kOutput, calls=%fused_computation.48 | convolution fusion | flops 6442450944 | bytes 24641536 | tf_op jit(solution)/shard_map/dot_general | solution.py:84
  299.7 1.1 reshape.170
  300.8 1.5 copy.159
  302.4 1.0 constant_dynamic-slice_fusion.2
  303.3 0.9 copy.178
  304.3 1.7 copy.158
  305.9 1.1 copy.160
  307.1 32.3 %all_to_all.60 = bf16[4,128,1280]{2,1,0:T(8,128)(2,1)S(1)} all-to-all(bf16[4,128,1280]{2,1,0:T(8,128)(2,1)S(1)} %pad_maximum_fusion.1), channel_id=1, replica_groups=mesh['groups'=2,'tensor'=4,'task'=4] {'task'}, dimensions={0} | all-to-all | bytes 2621440 | tf_op jit(solution)/shard_map/all_to_all | solution.py:31
  339.4 0.8 convolution_convert_fusion
  340.3 35.6 %all_to_all.61 = bf16[8,64,1280]{2,1,0:T(8,128)(2,1)S(1)} all-to-all(bf16[8,64,1280]{2,1,0:T(8,128)(2,1)S(1)} %bitcast.156), channel_id=1, replica_groups=mesh['groups'=2,'tensor'=4,'task'=4] {'groups','task'}, dimensions={0} | all-to-all | bytes 2621440 | tf_op jit(solution)/shard_map/all_to_all | solution.py:38
  375.8 0.7 slice.27
  376.6 2.0 copy.180
  378.5 1.9 copy.164
  380.4 2.0 copy.165
  382.4 4.1 all-to-all-start.7
  386.6 0.3 copy.185
  386.9 1.1 copy_bitcast_fusion.1
  388.0 4.6 %all-to-all-done.7 = bf16[64,8,256]{2,1,0:T(8,128)(2,1)} async-done(((bf16[64,8,256]{2,1,0:T(8,128)(2,1)}), bf16[64,8,256]{2,1,0:T(8,128)(2,1)}, u32[]{:S(2)}, u32[]{:S(2)}) %all-to-all-start.7) | async-done | bytes 262176 | tf_op jit(solution)/shard_map/all_to_all | solution.py:122
  392.6 3.5 all-to-all-start.6
  396.1 1.2 copy.192
  397.3 13.2 %all-to-all-done.6 = bf16[64,8,1024]{2,1,0:T(8,128)(2,1)S(1)} async-done(((bf16[64,8,1024]{2,1,0:T(8,128)(2,1)}), bf16[64,8,1024]{2,1,0:T(8,128)(2,1)S(1)}, u32[]{:S(2)}, u32[]{:S(2)}) %all-to-all-start.6) | async-done | bytes 1048608 | tf_op jit(solution)/shard_map/all_to_all | solution.py:122
  410.5 0.9 copy.191
  411.4 0.4 copy.186
  411.8 0.3 copy-done.1
  412.1 0.3 copy.181
  412.4 1.3 copy-done.2
  413.7 0.3 copy.182
  414.0 2.3 pad_maximum_fusion
  416.3 0.9 fusion.19
  417.4 2.1 fusion.3
  419.4 3.2 fusion.1
  (39 shorter events, 1.1 us)
Async XLA Ops:
  7.2 292.4 %copy-start = (bf16[128,8,1024]{2,1,0:T(8,128)(2,1)S(1)}, bf16[128,8,1024]{2,1,0:T(8,128)(2,1)}, u32[]{:S(2)}) copy-start(bf16[128,8,1024]{2,1,0:T(8,128)(2,1)} %param.14) | copy-start | bytes 6291460
  25.4 54.6 %all-to-all-start = ((bf16[4,128,2048]{1,2,0:T(8,128)(2,1)}), bf16[4,128,2048]{1,2,0:T(8,128)(2,1)}, u32[]{:S(2)}, u32[]{:S(2)}) async-start(bf16[4,128,2048]{1,2,0:T(8,128)(2,1)} %bitcast.137), calls=%async_computation.1 | async-start | bytes 4194304 | tf_op jit(solution)/shard_map/all_to_all | solution.py:31
  80.0 4.6 %copy-start.6 = (bf16[1024,512]{1,0:T(8,128)(2,1)S(1)}, bf16[1024,512]{1,0:T(8,128)(2,1)}, u32[]{:S(2)}) copy-start(bf16[1024,512]{1,0:T(8,128)(2,1)} %param.12) | copy-start | bytes 3145732
  80.0 4.6 %copy-start.7 = (bf16[64,1024]{1,0:T(8,128)(2,1)S(1)}, bf16[64,1024]{1,0:T(8,128)(2,1)}, u32[]{:S(2)}) copy-start(bf16[64,1024]{1,0:T(8,128)(2,1)} %param.11) | copy-start | bytes 393220
  80.0 86.1 %all-to-all-start.2 = ((bf16[4,128,2048]{1,2,0:T(8,128)(2,1)}), bf16[4,128,2048]{1,2,0:T(8,128)(2,1)}, u32[]{:S(2)}, u32[]{:S(2)}) async-start(bf16[4,128,2048]{1,2,0:T(8,128)(2,1)} %bitcast.136), calls=%async_computation.3 | async-start | bytes 4194304 | tf_op jit(solution)/shard_map/all_to_all | solution.py:31
  157.8 16.6 %copy-start.3 = (bf16[512,512]{1,0:T(8,128)(2,1)}, bf16[512,512]{1,0:T(8,128)(2,1)S(1)}, u32[]{:S(2)}) copy-start(bf16[512,512]{1,0:T(8,128)(2,1)S(1)} %all_gather.3) | copy-start | bytes 1572868
  166.1 48.5 %all-to-all-start.1 = ((bf16[8,64,2048]{2,1,0:T(8,128)(2,1)}), bf16[8,64,2048]{2,1,0:T(8,128)(2,1)}, u32[]{:S(2)}, u32[]{:S(2)}) async-start(bf16[8,64,2048]{2,1,0:T(8,128)(2,1)} %bitcast.150), calls=%async_computation.2 | async-start | bytes 4194304 | tf_op jit(solution)/shard_map/all_to_all | solution.py:38
  214.6 4.7 %copy-start.5 = (s32[64]{0:T(128)S(1)}, s32[64]{0:T(128)}, u32[]{:S(2)}) copy-start(s32[64]{0:T(128)} %param.10) | copy-start | bytes 772
  214.6 51.2 %all-to-all-start.3 = ((bf16[8,64,2048]{2,1,0:T(8,128)(2,1)}), bf16[8,64,2048]{2,1,0:T(8,128)(2,1)}, u32[]{:S(2)}, u32[]{:S(2)}) async-start(bf16[8,64,2048]{2,1,0:T(8,128)(2,1)} %bitcast.149), calls=%async_computation.4 | async-start | bytes 4194304 | tf_op jit(solution)/shard_map/all_to_all | solution.py:38
  219.1 197.2 %reduce-scatter.10.cloned.1.call-start = ((), (), s32[]{:S(2)}) async-start(), calls=%async_computation.13 | async-start | bytes 245760
  281.2 136.1 %reduce-scatter.8.cloned.1.call-start = ((), (), s32[]{:S(2)}) async-start(), calls=%async_computation.12 | async-start | bytes 1966080 | tf_op jit(solution)/shard_map/reduce_scatter | solution.py:87
  286.9 132.5 %reduce-scatter.6.cloned.1.call-start = ((), (), s32[]{:S(2)}) async-start(), calls=%async_computation.11 | async-start | bytes 7864320 | tf_op jit(solution)/shard_map/reduce_scatter | solution.py:83
  307.0 32.4 %copy-start.4 = (bf16[512,512]{1,0:T(8,128)(2,1)S(1)}, bf16[512,512]{1,0:T(8,128)(2,1)}, u32[]{:S(2)}) copy-start(bf16[512,512]{1,0:T(8,128)(2,1)} %copy-done.3) | copy-start | bytes 1572868
  382.4 10.2 %all-to-all-start.7 = ((bf16[64,8,256]{2,1,0:T(8,128)(2,1)}), bf16[64,8,256]{2,1,0:T(8,128)(2,1)}, u32[]{:S(2)}, u32[]{:S(2)}) async-start(bf16[64,8,256]{2,1,0:T(8,128)(2,1)} %copy.165), calls=%async_computation.9 | async-start | bytes 524288 | tf_op jit(solution)/shard_map/all_to_all | solution.py:122
  392.6 18.0 %all-to-all-start.6 = ((bf16[64,8,1024]{2,1,0:T(8,128)(2,1)}), bf16[64,8,1024]{2,1,0:T(8,128)(2,1)S(1)}, u32[]{:S(2)}, u32[]{:S(2)}) async-start(bf16[64,8,1024]{2,1,0:T(8,128)(2,1)} %copy_bitcast_fusion.1), calls=%async_computation.7 | async-start | bytes 2097152 | tf_op jit(solution)/shard_map/all_to_all | solution.py:122
  410.5 1.6 copy-start.1
  412.1 1.6 copy-start.2
Sparse Core Ops, SparseCore 0:
  281.4 17.0 reduce-scatter.9
  301.0 28.1 reduce-scatter.7
  331.9 58.3 reduce-scatter.5

commit v2 on v1

--- a/solution.py
+++ b/solution.py
@@ -32,9 +32,12 @@
     return got.reshape(-1, got.shape[2])
 
 
-def emit(every_hidden, matrix, n_owners):
+def produce(every_hidden, matrix, n_owners):
     made = jnp.dot(every_hidden, matrix, preferred_element_type=jnp.float32)
-    made = made.astype(jnp.bfloat16).reshape(n_owners, -1, matrix.shape[1])
+    return made.astype(jnp.bfloat16).reshape(n_owners, -1, matrix.shape[1])
+
+
+def to_owners(made):
     return lax.all_to_all(
         made, ("groups", "task"), split_axis=0, concat_axis=0, tiled=True
     )
@@ -68,33 +71,49 @@
     block_rows = rows // blocks
     block_tasks = task_counts.shape[0] // blocks
 
-    low, high = down_factor_head[:, :rank], down_factor_head[:, rank:]
-    down0 = regroup(pack_head(low, n_groups, n_task))
-    down1 = regroup(pack_head(high, n_groups, n_task))
+    after = lax.optimization_barrier
+
     packed_query = pack_head(query_up_head, n_groups, n_task)
     packed_value = pack_head(value_up_head, n_groups, n_task)
-    up = regroup(jnp.concatenate((packed_query, packed_value), axis=2))
+    packed_up = jnp.concatenate((packed_query, packed_value), axis=2)
+    flat_query = packed_query.shape[2]
+    up = regroup(packed_up)
 
     hidden = jax.nn.silu(
         jnp.dot(task_embeddings, embedding_weight, preferred_element_type=jnp.float32)
     ).astype(jnp.bfloat16)
     every_hidden = lax.all_gather(hidden, ("groups", "task"), axis=0, tiled=True)
 
-    base_query = lax.psum_scatter(
-        jnp.dot(tokens, w_query, preferred_element_type=jnp.float32),
-        "tensor", scatter_dimension=0, tiled=True,
+    packed0 = pack_head(down_factor_head[:, :rank], n_groups, n_task)
+    packed0, up, every_hidden = after((packed0, up, every_hidden))
+    down0 = regroup(packed0)
+
+    sums_query = jnp.dot(tokens, w_query, preferred_element_type=jnp.float32)
+    sums_value = jnp.dot(tokens, w_value, preferred_element_type=jnp.float32)
+    packed1 = pack_head(down_factor_head[:, rank:], n_groups, n_task)
+    made_up = produce(every_hidden, up, n_owners)
+    packed1, down0, sums_query, sums_value, made_up = after(
+        (packed1, down0, sums_query, sums_value, made_up)
     )
-    base_value = lax.psum_scatter(
-        jnp.dot(tokens, w_value, preferred_element_type=jnp.float32),
-        "tensor", scatter_dimension=0, tiled=True,
-    )
+    base_query = lax.psum_scatter(sums_query, "tensor", scatter_dimension=0, tiled=True)
+    base_value = lax.psum_scatter(sums_value, "tensor", scatter_dimension=0, tiled=True)
+    down1 = regroup(packed1)
 
-    half0 = unpack_factor(emit(every_hidden, down0, n_owners), rank)
-    half1 = unpack_factor(emit(every_hidden, down1, n_owners), rank)
-    got_up = emit(every_hidden, up, n_owners)
-    flat_query = packed_query.shape[2]
+    made0 = produce(every_hidden, down0, n_owners)
+    made_up, made0, down1 = after((made_up, made0, down1))
+    got_up = to_owners(made_up)
+    made1 = produce(every_hidden, down1, n_owners)
+    made0, made1, got_up = after((made0, made1, got_up))
+    every_up = lax.all_gather(got_up, "tensor", axis=0, tiled=False)
+    got0 = to_owners(made0)
     query_up_factors = unpack_factor(got_up[:, :, :flat_query], rank)
     value_up_factors = unpack_factor(got_up[:, :, flat_query:], rank)
+    made1, got0, base_query, base_value, query_up_factors, value_up_factors = after(
+        (made1, got0, base_query, base_value, query_up_factors, value_up_factors)
+    )
+    got1 = to_owners(made1)
+    half0 = unpack_factor(got0, rank)
+    half1 = unpack_factor(got1, rank)
     down_factors = jnp.concatenate((half0, half1), axis=1)
 
     member = block_member(task_counts, blocks, block_tasks, block_rows)
@@ -117,17 +136,26 @@
         member, lax.axis_index("tensor"), axis=0, keepdims=False
     )
 
+    own_up = lax.dynamic_slice_in_dim(
+        every_up, lax.axis_index("tensor") * block_tasks, block_tasks, axis=2
+    )
+
     def delta(part, factors):
         spread = (own_member[:, :, None] * part[:, None, :]).reshape(block_rows, -1)
-        whole = lax.all_to_all(factors, "tensor", split_axis=0, concat_axis=2, tiled=True)
+        columns = factors.shape[3] // rank
+        whole = factors.reshape(-1, block_tasks, rank, columns).transpose(1, 2, 0, 3)
         return jnp.dot(
             spread,
             whole.reshape(block_tasks * rank, -1).astype(jnp.float32),
             precision=lax.Precision.HIGHEST,
         )
 
-    query = base_query + ADAPTER_SCALE * delta(low_rank[:, :rank], query_up_factors)
-    value = base_value + ADAPTER_SCALE * delta(low_rank[:, rank:], value_up_factors)
+    query = base_query + ADAPTER_SCALE * delta(
+        low_rank[:, :rank], own_up[..., :flat_query]
+    )
+    value = base_value + ADAPTER_SCALE * delta(
+        low_rank[:, rank:], own_up[..., flat_query:]
+    )
     return (
         query.astype(jnp.bfloat16),
         value.astype(jnp.bfloat16),

time: 431 us -> 366 us (0.85)
  blocking collectives: 141 us -> 46.9 us
  waiting for transfers between devices: 126 us -> 167 us
  local copies, waits for them, and re-layouts: 79.5 us -> 64 us
    all_to_all x2 -> x0, blocking collectives: 67.8 us -> none  [the longest x1 35.6 us: emit(): lax.all_to_all(made, ('groups', 'task'), split_axis=0, concat_axis=0, til...]
    all_gather x1, blocking collectives: 72.8 us -> 46.9 us  [local(): lax.all_gather(hidden, ('groups', 'task'), axis=0, tiled=True)]
    all_to_all x2 -> x3, waiting for transfers between devices: 41 us -> 58 us  [regroup(): lax.all_to_all(packed, 'task', split_axis=0, concat_axis=0, tiled=True)]
    unnamed x4 -> x5, waiting for transfers between devices: 0.05 us -> 13.2 us
    all_to_all x4 -> x3, waiting for transfers between devices: 85.2 us -> 96.1 us  [to_owners(): lax.all_to_all(made, ('groups', 'task'), split_axis=0, concat_axis=0, til...]
    all_to_all x4 -> x3, starting transfers between devices: 16.4 us -> 12.7 us  [to_owners(): lax.all_to_all(made, ('groups', 'task'), split_axis=0, concat_axis=0, til...]
    unnamed x30 -> x33, local copies, waits for them, and re-layouts: 22.4 us -> 19 us
    all_to_all x2 -> x3, starting transfers between devices: 10.9 us -> 13.8 us  [regroup(): lax.all_to_all(packed, 'task', split_axis=0, concat_axis=0, tiled=True)]
  transfers between devices with their start and end apart: 9 -> 10, of which waited for: 5 -> 6; matrix products, arithmetic and copies ran while one was open for 19% -> 22% of each run, Pallas kernels for 0% -> 0%
where the time goes in v2:
time: 366 us; the launch traced here: 364 us
  waiting for transfers between devices  167 us (46%)
  local copies, waits for them, and re-layouts  64 us (17%)
  blocking collectives  46.9 us (13%)
  matrix products  39.1 us (11%)
  starting transfers between devices  26.7 us (7%)
  between operations  14.2 us (4%)
  other arithmetic  6.24 us (2%)
    all_to_all x3, waiting for transfers between devices, to_owners(): lax.all_to_all(made, ('groups', 'task'), split_axis=0, concat_axis=0, til...  96.1 us
    all_to_all x3, waiting for transfers between devices, regroup(): lax.all_to_all(packed, 'task', split_axis=0, concat_axis=0, tiled=True)  58 us
    all_gather x1, blocking collectives, local(): lax.all_gather(hidden, ('groups', 'task'), axis=0, tiled=True)  46.9 us
    unnamed x33, local copies, waits for them, and re-layouts  19 us
    all_to_all x3, starting transfers between devices, regroup(): lax.all_to_all(packed, 'task', split_axis=0, concat_axis=0, tiled=True)  13.8 us
    unnamed x5, waiting for transfers between devices  13.2 us
    all_to_all x3, starting transfers between devices, to_owners(): lax.all_to_all(made, ('groups', 'task'), split_axis=0, concat_axis=0, til...  12.7 us
    dot_general x1, matrix products, local(): sums_query = jnp.dot(tokens, w_query, preferred_element_type=jnp.float32)  12.3 us
  transfers between devices with their start and end apart: 10, of which 6 were waited for; matrix products, arithmetic and copies ran while one was open for 22% of the time, Pallas kernels for 0%

profile of v2, /device:TPU:0, one launch (start us, length us, event | category | flops | bytes accessed | tf_op | source)
XLA Modules:
  0.0 364.5 jit_solution(1181964810561942000)
XLA Ops:
  7.2 1.6 copy-done
  8.9 0.3 reshape.165
  9.2 0.3 copy.149
  9.5 0.7 copy-done.6
  10.2 0.2 copy.172
  10.6 1.2 pad_maximum_fusion.1
  11.8 6.3 %all-to-all-start = ((bf16[4,128,1280]{2,1,0:T(8,128)(2,1)}), bf16[4,128,1280]{2,1,0:T(8,128)(2,1)S(1)}, u32[]{:S(2)}, u32[]{:S(2)}) async-start(bf16[4,128,1280]{2,1,0:T(8,128)(2,1)} %pad_maximum_fusion.1), calls=%async_computation | async-start | bytes 2621440 | tf_op jit(solution)/shard_map/all_to_all | solution.py:31
  18.1 4.0 %fusion.20 = (bf16[128,8,2048]{2,1,0:T(8,128)(2,1)S(1)}, bf16[128,8,2048]{2,1,0:T(8,128)(2,1)S(1)}) fusion(bf16[128,16,2048]{2,1,0:T(8,128)(2,1)} %param.13), kind=kLoop, calls=%fused_computation.50 | loop fusion | bytes 16777216 | tf_op jit(solution)/shard_map/slice | solution.py:87
  22.1 2.5 constant_dynamic-slice_fusion.3
  24.6 3.3 copy.171
  28.0 1.6 copy.146
  29.6 0.3 multiply_convert_fusion
  29.9 46.9 %all_gather.9 = bf16[512,512]{1,0:T(8,128)(2,1)} all-gather(bf16[64,512]{1,0:T(8,128)(2,1)S(1)} %multiply_convert_fusion), channel_id=1, replica_groups=mesh['groups'=2,'tensor'=4,'task'=4] {'groups','task'}, dimensions={0}, use_global_device_ids=true | all-gather | bytes 589824 | tf_op jit(solution)/shard_map/all_gather | solution.py:85
  76.9 3.6 all-to-all-start.1
  80.5 4.1 %copy.169 = bf16[128,8,1024]{0,2,1:T(8,128)(2,1)} copy(bf16[128,8,1024]{2,1,0:T(8,128)(2,1)} %get-tuple-element.94) | data formatting | bytes 4194304
  84.7 3.3 copy.144
  88.0 5.1 %fusion.23 = f32[384,1024]{1,0:T(8,128)} fusion(bf16[384,2048]{1,0:T(8,128)(2,1)S(1)} %copy-done.4, bf16[2048,1024]{1,0:T(8,128)(2,1)} %param.17), kind=kOutput, calls=%fused_computation.53 | convolution fusion | flops 1610612736 | bytes 7340032 | tf_op jit(solution)/shard_map/dot_general | solution.py:92
  93.1 12.3 %fusion.22 = f32[384,4096]{1,0:T(8,128)} fusion(bf16[384,2048]{1,0:T(8,128)(2,1)} %param.9, bf16[2048,4096]{1,0:T(8,128)(2,1)} %param.16), kind=kOutput, calls=%fused_computation.52 | convolution fusion | flops 6442450944 | bytes 24641536 | tf_op jit(solution)/shard_map/dot_general | solution.py:91
  105.4 2.9 convolution_convert_fusion.2
  108.4 15.0 %all-to-all-done.1 = bf16[4,128,2048]{1,2,0:T(8,128)(2,1)S(1)} async-done(((bf16[4,128,2048]{1,2,0:T(8,128)(2,1)}), bf16[4,128,2048]{1,2,0:T(8,128)(2,1)S(1)}, u32[]{:S(2)}, u32[]{:S(2)}) %all-to-all-start.1) | async-done | bytes 2097184 | tf_op jit(solution)/shard_map/all_to_all | solution.py:31
  123.4 2.6 copy.151
  126.0 0.7 reduce-scatter.6.cloned.1.call-update
  126.7 3.9 %all-to-all-start.2 = ((bf16[4,128,2048]{1,2,0:T(8,128)(2,1)}), bf16[4,128,2048]{1,2,0:T(8,128)(2,1)S(1)}, u32[]{:S(2)}, u32[]{:S(2)}) async-start(bf16[4,128,2048]{1,2,0:T(8,128)(2,1)} %bitcast.2), calls=%async_computation.2 | async-start | bytes 4194304 | tf_op jit(solution)/shard_map/all_to_all | solution.py:31
  130.6 4.4 %convolution_convert_fusion.1 = bf16[512,2048]{1,0:T(8,128)(2,1)} fusion(bf16[512,512]{1,0:T(8,128)(2,1)S(1)} %copy-done.5, bf16[512,2048]{1,0:T(8,128)(2,1)} %bitcast.156), kind=kOutput, calls=%fused_computation.5 | convolution fusion | flops 1074790400 | bytes 4718592 | tf_op jit(solution)/shard_map/dot_general | solution.py:36
  135.1 43.0 %all-to-all-done.2 = bf16[4,128,2048]{1,2,0:T(8,128)(2,1)S(1)} async-done(((bf16[4,128,2048]{1,2,0:T(8,128)(2,1)}), bf16[4,128,2048]{1,2,0:T(8,128)(2,1)S(1)}, u32[]{:S(2)}, u32[]{:S(2)}) %all-to-all-start.2) | async-done | bytes 2097184 | tf_op jit(solution)/shard_map/all_to_all | solution.py:31
  178.0 2.6 copy.152
  180.6 3.6 all-to-all-start.3
  184.2 4.3 %convolution_convert_fusion = bf16[512,2048]{1,0:T(8,128)(2,1)} fusion(bf16[512,512]{1,0:T(8,128)(2,1)S(1)} %copy-done.5, bf16[512,2048]{1,0:T(8,128)(2,1)} %bitcast.157), kind=kOutput, calls=%fused_computation.4 | convolution fusion | flops 1074790400 | bytes 4718592 | tf_op jit(solution)/shard_map/dot_general | solution.py:36
  188.5 27.3 %all-to-all-done.3 = bf16[8,64,1280]{2,1,0:T(8,128)(2,1)S(1)} async-done(((bf16[8,64,1280]{2,1,0:T(8,128)(2,1)}), bf16[8,64,1280]{2,1,0:T(8,128)(2,1)S(1)}, u32[]{:S(2)}, u32[]{:S(2)}) %all-to-all-start.3) | async-done | bytes 1310752 | tf_op jit(solution)/shard_map/all_to_all | solution.py:41
  215.9 1.1 copy-done.2
  217.0 4.7 %all-to-all-start.4 = ((bf16[8,64,2048]{2,1,0:T(8,128)(2,1)}), bf16[8,64,2048]{2,1,0:T(8,128)(2,1)}, u32[]{:S(2)}, u32[]{:S(2)}) async-start(bf16[8,64,2048]{2,1,0:T(8,128)(2,1)} %bitcast.155), calls=%async_computation.4 | async-start | bytes 4194304 | tf_op jit(solution)/shard_map/all_to_all | solution.py:41
  221.7 2.7 copy.154
  224.5 1.0 slice-done
  225.5 0.3 copy.177
  225.8 1.1 copy_bitcast_fusion.1
  226.9 41.9 %all-to-all-done.4 = bf16[8,64,2048]{2,1,0:T(8,128)(2,1)} async-done(((bf16[8,64,2048]{2,1,0:T(8,128)(2,1)}), bf16[8,64,2048]{2,1,0:T(8,128)(2,1)}, u32[]{:S(2)}, u32[]{:S(2)}) %all-to-all-start.4) | async-done | bytes 2097184 | tf_op jit(solution)/shard_map/all_to_all | solution.py:41
  268.9 4.5 %all-to-all-start.5 = ((bf16[8,64,2048]{2,1,0:T(8,128)(2,1)}), bf16[8,64,2048]{2,1,0:T(8,128)(2,1)}, u32[]{:S(2)}, u32[]{:S(2)}) async-start(bf16[8,64,2048]{2,1,0:T(8,128)(2,1)} %bitcast.154), calls=%async_computation.7 | async-start | bytes 4194304 | tf_op jit(solution)/shard_map/all_to_all | solution.py:41
  273.8 2.3 copy.178
  276.1 0.5 bitcast_bitcast_fusion.2
  276.5 1.6 copy.175
  278.1 3.6 copy.156
  281.7 2.9 reshape_reshape.6
  284.6 2.1 fusion.6
  286.8 1.0 copy.164
  287.8 1.0 constant_dynamic-slice_fusion.1
  288.8 0.4 reshape.185
  289.2 0.7 copy.161
  289.9 1.1 reshape.186
  291.0 1.3 constant_dynamic-slice_fusion
  292.3 0.3 copy.180
  292.7 0.7 copy.188
  293.4 26.9 %all-to-all-done.5 = bf16[8,64,2048]{2,1,0:T(8,128)(2,1)} async-done(((bf16[8,64,2048]{2,1,0:T(8,128)(2,1)}), bf16[8,64,2048]{2,1,0:T(8,128)(2,1)}, u32[]{:S(2)}, u32[]{:S(2)}) %all-to-all-start.5) | async-done | bytes 2097184 | tf_op jit(solution)/shard_map/all_to_all | solution.py:41
  320.3 2.3 copy.179
  322.6 0.5 bitcast_bitcast_fusion
  323.0 1.6 copy.176
  324.6 3.6 copy.158
  328.2 2.9 reshape_reshape.7
  331.1 2.1 fusion.7
  333.3 0.8 copy.166
  334.1 4.8 %pad_maximum_fusion = bf16[64,16,2048]{2,1,0:T(8,128)(2,1)} fusion(bf16[64,8,2048]{2,1,0:T(8,128)(2,1)} %bitcast.145, bf16[64,8,2048]{2,1,0:T(8,128)(2,1)} %bitcast.144), kind=kLoop, calls=%fused_computation.3 | loop fusion | flops 8388608 | bytes 8388608 | tf_op jit(solution)/shard_map/concatenate | solution.py:117
  339.0 12.4 %reduce-scatter.10.cloned.1.call-done = f32[96,16]{1,0:T(8,128)} async-done(((f32[384,16]{1,0:T(8,128)}), f32[96,16]{1,0:T(8,128)}) %reduce-scatter.10.cloned.1.call-update) | async-done | bytes 6160
  351.4 0.9 fusion.21
  352.4 2.2 fusion.3
  354.7 3.3 fusion.1
  (49 shorter events, 1.5 us)
Async XLA Ops:
  7.2 1.6 copy-start
  9.2 1.0 copy-start.6
  11.8 65.1 %all-to-all-start = ((bf16[4,128,1280]{2,1,0:T(8,128)(2,1)}), bf16[4,128,1280]{2,1,0:T(8,128)(2,1)S(1)}, u32[]{:S(2)}, u32[]{:S(2)}) async-start(bf16[4,128,1280]{2,1,0:T(8,128)(2,1)} %pad_maximum_fusion.1), calls=%async_computation | async-start | bytes 2621440 | tf_op jit(solution)/shard_map/all_to_all | solution.py:31
  27.9 1.6 copy-start.8
  27.9 1.6 copy-start.9
  76.9 46.5 %all-to-all-start.1 = ((bf16[4,128,2048]{1,2,0:T(8,128)(2,1)}), bf16[4,128,2048]{1,2,0:T(8,128)(2,1)S(1)}, u32[]{:S(2)}, u32[]{:S(2)}) async-start(bf16[4,128,2048]{1,2,0:T(8,128)(2,1)} %bitcast.5), calls=%async_computation.1 | async-start | bytes 4194304 | tf_op jit(solution)/shard_map/all_to_all | solution.py:31
  80.5 146.4 %reduce-scatter.8.cloned.1.call-start = ((), (), s32[]{:S(2)}) async-start(), calls=%async_computation.10 | async-start | bytes 1966080 | tf_op jit(solution)/shard_map/reduce_scatter | solution.py:99
  84.7 3.3 copy-start.4
  126.0 142.9 %reduce-scatter.6.cloned.1.call-start = ((), (), s32[]{:S(2)}) async-start(), calls=%async_computation.9 | async-start | bytes 7864320 | tf_op jit(solution)/shard_map/reduce_scatter | solution.py:98
  126.7 3.9 %copy-start.5 = (bf16[512,512]{1,0:T(8,128)(2,1)S(1)}, bf16[512,512]{1,0:T(8,128)(2,1)}, u32[]{:S(2)}) copy-start(bf16[512,512]{1,0:T(8,128)(2,1)} %all_gather.9) | copy-start | bytes 1572868
  126.7 51.3 %all-to-all-start.2 = ((bf16[4,128,2048]{1,2,0:T(8,128)(2,1)}), bf16[4,128,2048]{1,2,0:T(8,128)(2,1)S(1)}, u32[]{:S(2)}, u32[]{:S(2)}) async-start(bf16[4,128,2048]{1,2,0:T(8,128)(2,1)} %bitcast.2), calls=%async_computation.2 | async-start | bytes 4194304 | tf_op jit(solution)/shard_map/all_to_all | solution.py:31
  180.6 35.2 %all-to-all-start.3 = ((bf16[8,64,1280]{2,1,0:T(8,128)(2,1)}), bf16[8,64,1280]{2,1,0:T(8,128)(2,1)S(1)}, u32[]{:S(2)}, u32[]{:S(2)}) async-start(bf16[8,64,1280]{2,1,0:T(8,128)(2,1)} %bitcast.13), calls=%async_computation.3 | async-start | bytes 2621440 | tf_op jit(solution)/shard_map/all_to_all | solution.py:41
  184.2 103.6 %all-gather.3.cloned.1.call-start = ((), (), s32[]{:S(2)}) async-start(), calls=%async_computation.11 | async-start | bytes 6553600 | tf_op jit(solution)/shard_map/all_gather | solution.py:107
  215.9 1.1 copy-start.2
  217.0 4.7 %copy-start.3 = (bf16[8,64,1280]{2,1,0:T(8,128)(2,1)S(1)}, bf16[8,64,1280]{2,1,0:T(8,128)(2,1)}, u32[]{:S(2)}) copy-start(bf16[8,64,1280]{2,1,0:T(8,128)(2,1)} %copy-done.2) | copy-start | bytes 3932164
  217.0 51.9 %all-to-all-start.4 = ((bf16[8,64,2048]{2,1,0:T(8,128)(2,1)}), bf16[8,64,2048]{2,1,0:T(8,128)(2,1)}, u32[]{:S(2)}, u32[]{:S(2)}) async-start(bf16[8,64,2048]{2,1,0:T(8,128)(2,1)} %bitcast.155), calls=%async_computation.4 | async-start | bytes 4194304 | tf_op jit(solution)/shard_map/all_to_all | solution.py:41
  224.4 1.1 slice-start
  268.9 4.5 %copy-start.7 = (s32[64]{0:T(128)S(1)}, s32[64]{0:T(128)}, u32[]{:S(2)}) copy-start(s32[64]{0:T(128)} %param.10) | copy-start | bytes 772
  268.9 51.4 %all-to-all-start.5 = ((bf16[8,64,2048]{2,1,0:T(8,128)(2,1)}), bf16[8,64,2048]{2,1,0:T(8,128)(2,1)}, u32[]{:S(2)}, u32[]{:S(2)}) async-start(bf16[8,64,2048]{2,1,0:T(8,128)(2,1)} %bitcast.154), calls=%async_computation.7 | async-start | bytes 4194304 | tf_op jit(solution)/shard_map/all_to_all | solution.py:41
  273.4 78.0 %reduce-scatter.10.cloned.1.call-start = ((), (), s32[]{:S(2)}) async-start(), calls=%async_computation.12 | async-start | bytes 245760
  352.4 5.6 %copy-start.1 = (bf16[128,8,1024]{2,1,0:T(8,128)(2,1)S(1)}, bf16[128,8,1024]{2,1,0:T(8,128)(2,1)}, u32[]{:S(2)}) copy-start(bf16[128,8,1024]{2,1,0:T(8,128)(2,1)} %param.14) | copy-start | bytes 6291460
Sparse Core Ops, SparseCore 0:
  126.1 26.2 reduce-scatter.7
  155.1 58.3 reduce-scatter.5
  217.1 38.4 all-gather.2
  334.3 17.0 reduce-scatter.9

commit v3 on v2

--- a/solution.py
+++ b/solution.py
@@ -43,6 +43,10 @@
     )
 
 
+def corner(array):
+    return lax.slice(array, (0,) * array.ndim, (1,) * array.ndim)
+
+
 def unpack_factor(got, ranks):
     owners, tasks, flat = got.shape
     return (
@@ -77,15 +81,17 @@
     packed_value = pack_head(value_up_head, n_groups, n_task)
     packed_up = jnp.concatenate((packed_query, packed_value), axis=2)
     flat_query = packed_query.shape[2]
-    up = regroup(packed_up)
 
     hidden = jax.nn.silu(
         jnp.dot(task_embeddings, embedding_weight, preferred_element_type=jnp.float32)
     ).astype(jnp.bfloat16)
-    every_hidden = lax.all_gather(hidden, ("groups", "task"), axis=0, tiled=True)
+    every_hidden = to_owners(jnp.broadcast_to(hidden, (n_owners, *hidden.shape)))
+    packed_up, _ = after((packed_up, corner(every_hidden)))
+    every_hidden = every_hidden.reshape(-1, hidden.shape[1])
+    up = regroup(packed_up)
 
     packed0 = pack_head(down_factor_head[:, :rank], n_groups, n_task)
-    packed0, up, every_hidden = after((packed0, up, every_hidden))
+    packed0, every_hidden, up = after((packed0, every_hidden, up))
     down0 = regroup(packed0)
 
     sums_query = jnp.dot(tokens, w_query, preferred_element_type=jnp.float32)
@@ -100,7 +106,7 @@
     down1 = regroup(packed1)
 
     made0 = produce(every_hidden, down0, n_owners)
-    made_up, made0, down1 = after((made_up, made0, down1))
+    made_up, made0, _ = after((made_up, made0, corner(down1)))
     got_up = to_owners(made_up)
     made1 = produce(every_hidden, down1, n_owners)
     made0, made1, got_up = after((made0, made1, got_up))

time: 366 us -> 359 us (0.981)
  blocking collectives: 46.9 us -> 0 us
  waiting for transfers between devices: 167 us -> 197 us
  starting transfers between devices: 26.7 us -> 31 us
  local copies, waits for them, and re-layouts: 64 us -> 67.9 us
    all_gather x1 -> x0, blocking collectives: 46.9 us -> none  [local(): lax.all_gather(hidden, ('groups', 'task'), axis=0, tiled=True)]
    all_to_all x3, waiting for transfers between devices: 58 us -> 81.5 us  [regroup(): lax.all_to_all(packed, 'task', split_axis=0, concat_axis=0, tiled=True)]
    all_to_all x3 -> x4, starting transfers between devices: 12.7 us -> 20 us  [to_owners(): lax.all_to_all(made, ('groups', 'task'), split_axis=0, concat_axis=0, til...]
    all_to_all x3 -> x4, waiting for transfers between devices: 96.1 us -> 102 us  [to_owners(): lax.all_to_all(made, ('groups', 'task'), split_axis=0, concat_axis=0, til...]
    unnamed x33 -> x29, local copies, waits for them, and re-layouts: 19 us -> 19.8 us
  transfers between devices with their start and end apart: 10 -> 11, of which waited for: 6 -> 8; matrix products, arithmetic and copies ran while one was open for 22% -> 24% of each run, Pallas kernels for 0% -> 0%
where the time goes in v3:
time: 359 us; the launch traced here: 357 us
  waiting for transfers between devices  197 us (55%)
  local copies, waits for them, and re-layouts  67.9 us (19%)
  matrix products  40.9 us (11%)
  starting transfers between devices  31 us (9%)
  between operations  14.1 us (4%)
  other arithmetic  6.24 us (2%)
    all_to_all x4, waiting for transfers between devices, to_owners(): lax.all_to_all(made, ('groups', 'task'), split_axis=0, concat_axis=0, til...  102 us
    all_to_all x3, waiting for transfers between devices, regroup(): lax.all_to_all(packed, 'task', split_axis=0, concat_axis=0, tiled=True)  81.5 us
    all_to_all x4, starting transfers between devices, to_owners(): lax.all_to_all(made, ('groups', 'task'), split_axis=0, concat_axis=0, til...  20 us
    unnamed x29, local copies, waits for them, and re-layouts  19.8 us
    unnamed x5, waiting for transfers between devices  13.2 us
    dot_general x1, matrix products, local(): sums_query = jnp.dot(tokens, w_query, preferred_element_type=jnp.float32)  12.3 us
    dot_general x3, matrix products, produce(): made = jnp.dot(every_hidden, matrix, preferred_element_type=jnp.float32)  12.1 us
    all_to_all x3, starting transfers between devices, regroup(): lax.all_to_all(packed, 'task', split_axis=0, concat_axis=0, tiled=True)  10.8 us
  transfers between devices with their start and end apart: 11, of which 8 were waited for; matrix products, arithmetic and copies ran while one was open for 24% of the time, Pallas kernels for 0%

profile of v3, /device:TPU:0, one launch (start us, length us, event | category | flops | bytes accessed | tf_op | source)
XLA Modules:
  0.0 357.3 jit_solution(2353532319620679471)
XLA Ops:
  7.2 1.8 multiply_convert_fusion
  8.9 0.8 broadcast_in_dim.24
  9.8 7.3 %all-to-all-start = ((bf16[8,64,512]{2,1,0:T(8,128)(2,1)}), bf16[8,64,512]{2,1,0:T(8,128)(2,1)}, u32[]{:S(2)}, u32[]{:S(2)}) async-start(bf16[8,64,512]{2,1,0:T(8,128)(2,1)} %broadcast_in_dim.24), calls=%async_computation | async-start | bytes 1048576 | tf_op jit(solution)/shard_map/all_to_all | solution.py:41
  17.5 0.3 copy.149
  17.8 0.7 copy-done.6
  19.0 1.2 pad_maximum_fusion.1
  20.1 12.4 %all-to-all-done = bf16[8,64,512]{2,1,0:T(8,128)(2,1)} async-done(((bf16[8,64,512]{2,1,0:T(8,128)(2,1)}), bf16[8,64,512]{2,1,0:T(8,128)(2,1)}, u32[]{:S(2)}, u32[]{:S(2)}) %all-to-all-start) | async-done | bytes 524320 | tf_op jit(solution)/shard_map/all_to_all | solution.py:41
  32.6 3.5 all-to-all-start.1
  36.1 4.0 %fusion.20 = (bf16[128,8,2048]{2,1,0:T(8,128)(2,1)S(1)}, bf16[128,8,2048]{2,1,0:T(8,128)(2,1)S(1)}) fusion(bf16[128,16,2048]{2,1,0:T(8,128)(2,1)} %param.13), kind=kLoop, calls=%fused_computation.50 | loop fusion | bytes 16777216 | tf_op jit(solution)/shard_map/slice | solution.py:93
  40.1 2.5 constant_dynamic-slice_fusion.3
  42.6 3.3 copy.171
  45.9 1.6 copy.146
  47.5 18.7 %all-to-all-done.1 = bf16[4,128,1280]{2,1,0:T(8,128)(2,1)S(1)} async-done(((bf16[4,128,1280]{2,1,0:T(8,128)(2,1)}), bf16[4,128,1280]{2,1,0:T(8,128)(2,1)S(1)}, u32[]{:S(2)}, u32[]{:S(2)}) %all-to-all-start.1) | async-done | bytes 1310752 | tf_op jit(solution)/shard_map/all_to_all | solution.py:31
  66.2 3.6 %all-to-all-start.2 = ((bf16[4,128,2048]{1,2,0:T(8,128)(2,1)}), bf16[4,128,2048]{1,2,0:T(8,128)(2,1)S(1)}, u32[]{:S(2)}, u32[]{:S(2)}) async-start(bf16[4,128,2048]{1,2,0:T(8,128)(2,1)} %bitcast.5), calls=%async_computation.2 | async-start | bytes 4194304 | tf_op jit(solution)/shard_map/all_to_all | solution.py:31
  69.9 4.1 %copy.169 = bf16[128,8,1024]{0,2,1:T(8,128)(2,1)} copy(bf16[128,8,1024]{2,1,0:T(8,128)(2,1)} %get-tuple-element.92) | data formatting | bytes 4194304
  74.0 3.3 copy.144
  77.3 5.1 %fusion.23 = f32[384,1024]{1,0:T(8,128)} fusion(bf16[384,2048]{1,0:T(8,128)(2,1)S(1)} %copy-done.5, bf16[2048,1024]{1,0:T(8,128)(2,1)} %param.17), kind=kOutput, calls=%fused_computation.53 | convolution fusion | flops 1610612736 | bytes 7340032 | tf_op jit(solution)/shard_map/dot_general | solution.py:98
  82.5 12.3 %fusion.22 = f32[384,4096]{1,0:T(8,128)} fusion(bf16[384,2048]{1,0:T(8,128)(2,1)} %param.9, bf16[2048,4096]{1,0:T(8,128)(2,1)} %param.16), kind=kOutput, calls=%fused_computation.52 | convolution fusion | flops 6442450944 | bytes 24641536 | tf_op jit(solution)/shard_map/dot_general | solution.py:97
  94.7 2.9 convolution_convert_fusion.2
  97.7 19.8 %all-to-all-done.2 = bf16[4,128,2048]{1,2,0:T(8,128)(2,1)S(1)} async-done(((bf16[4,128,2048]{1,2,0:T(8,128)(2,1)}), bf16[4,128,2048]{1,2,0:T(8,128)(2,1)S(1)}, u32[]{:S(2)}, u32[]{:S(2)}) %all-to-all-start.2) | async-done | bytes 2097184 | tf_op jit(solution)/shard_map/all_to_all | solution.py:31
  117.5 2.6 copy.151
  120.1 0.7 reduce-scatter.6.cloned.1.call-update
  120.8 3.7 %all-to-all-start.3 = ((bf16[4,128,2048]{1,2,0:T(8,128)(2,1)}), bf16[4,128,2048]{1,2,0:T(8,128)(2,1)S(1)}, u32[]{:S(2)}, u32[]{:S(2)}) async-start(bf16[4,128,2048]{1,2,0:T(8,128)(2,1)} %bitcast.2), calls=%async_computation.3 | async-start | bytes 4194304 | tf_op jit(solution)/shard_map/all_to_all | solution.py:31
  124.5 4.6 %convolution_convert_fusion.1 = bf16[512,2048]{1,0:T(8,128)(2,1)} fusion(bf16[512,512]{1,0:T(8,128)(2,1)} %bitcast.6, bf16[512,2048]{1,0:T(8,128)(2,1)} %bitcast.157), kind=kOutput, calls=%fused_computation.5 | convolution fusion | flops 1074790400 | bytes 4718592 | tf_op jit(solution)/shard_map/dot_general | solution.py:36
  129.1 43.0 %all-to-all-done.3 = bf16[4,128,2048]{1,2,0:T(8,128)(2,1)S(1)} async-done(((bf16[4,128,2048]{1,2,0:T(8,128)(2,1)}), bf16[4,128,2048]{1,2,0:T(8,128)(2,1)S(1)}, u32[]{:S(2)}, u32[]{:S(2)}) %all-to-all-start.3) | async-done | bytes 2097184 | tf_op jit(solution)/shard_map/all_to_all | solution.py:31
  172.1 1.3 copy-done.4
  173.4 3.6 all-to-all-start.4
  177.1 4.0 %copy.152 = bf16[4,128,2048]{2,1,0:T(8,128)(2,1)} copy(bf16[4,128,2048]{1,2,0:T(8,128)(2,1)} %copy-done.4) | data formatting | bytes 4194304 | tf_op jit(solution)/shard_map/all_to_all | solution.py:31
  181.0 4.5 %convolution_convert_fusion = bf16[512,2048]{1,0:T(8,128)(2,1)} fusion(bf16[512,512]{1,0:T(8,128)(2,1)} %bitcast.6, bf16[512,2048]{1,0:T(8,128)(2,1)} %bitcast.158), kind=kOutput, calls=%fused_computation.4 | convolution fusion | flops 1074790400 | bytes 4718592 | tf_op jit(solution)/shard_map/dot_general | solution.py:36
  185.6 23.1 %all-to-all-done.4 = bf16[8,64,1280]{2,1,0:T(8,128)(2,1)S(1)} async-done(((bf16[8,64,1280]{2,1,0:T(8,128)(2,1)}), bf16[8,64,1280]{2,1,0:T(8,128)(2,1)S(1)}, u32[]{:S(2)}, u32[]{:S(2)}) %all-to-all-start.4) | async-done | bytes 1310752 | tf_op jit(solution)/shard_map/all_to_all | solution.py:41
  208.7 1.1 copy-done.2
  209.8 4.7 %all-to-all-start.5 = ((bf16[8,64,2048]{2,1,0:T(8,128)(2,1)}), bf16[8,64,2048]{2,1,0:T(8,128)(2,1)}, u32[]{:S(2)}, u32[]{:S(2)}) async-start(bf16[8,64,2048]{2,1,0:T(8,128)(2,1)} %bitcast.156), calls=%async_computation.5 | async-start | bytes 4194304 | tf_op jit(solution)/shard_map/all_to_all | solution.py:41
  214.5 2.7 copy.154
  217.3 1.0 slice-done
  218.3 0.8 copy.155
  219.4 1.1 copy_bitcast_fusion.1
  220.6 41.1 %all-to-all-done.5 = bf16[8,64,2048]{2,1,0:T(8,128)(2,1)} async-done(((bf16[8,64,2048]{2,1,0:T(8,128)(2,1)}), bf16[8,64,2048]{2,1,0:T(8,128)(2,1)}, u32[]{:S(2)}, u32[]{:S(2)}) %all-to-all-start.5) | async-done | bytes 2097184 | tf_op jit(solution)/shard_map/all_to_all | solution.py:41
  261.7 4.5 %all-to-all-start.6 = ((bf16[8,64,2048]{2,1,0:T(8,128)(2,1)}), bf16[8,64,2048]{2,1,0:T(8,128)(2,1)}, u32[]{:S(2)}, u32[]{:S(2)}) async-start(bf16[8,64,2048]{2,1,0:T(8,128)(2,1)} %bitcast.155), calls=%async_computation.8 | async-start | bytes 4194304 | tf_op jit(solution)/shard_map/all_to_all | solution.py:41
  266.6 1.0 constant_dynamic-slice_fusion.1
  267.6 0.4 reshape.189
  268.0 0.7 copy.161
  268.7 1.1 reshape.190
  269.8 1.3 constant_dynamic-slice_fusion
  271.6 0.7 copy.188
  272.3 2.3 copy.178
  274.5 0.5 bitcast_bitcast_fusion.2
  275.0 1.6 copy.175
  276.6 3.6 copy.156
  280.2 2.9 reshape_reshape.6
  283.1 2.1 fusion.6
  285.3 2.0 copy.164
  287.3 25.8 %all-to-all-done.6 = bf16[8,64,2048]{2,1,0:T(8,128)(2,1)} async-done(((bf16[8,64,2048]{2,1,0:T(8,128)(2,1)}), bf16[8,64,2048]{2,1,0:T(8,128)(2,1)}, u32[]{:S(2)}, u32[]{:S(2)}) %all-to-all-start.6) | async-done | bytes 2097184 | tf_op jit(solution)/shard_map/all_to_all | solution.py:41
  313.1 2.3 copy.179
  315.4 0.5 bitcast_bitcast_fusion
  315.9 1.6 copy.176
  317.4 3.6 copy.158
  321.0 2.9 reshape_reshape.7
  323.9 2.1 fusion.7
  326.1 0.8 copy.166
  327.0 4.8 %pad_maximum_fusion = bf16[64,16,2048]{2,1,0:T(8,128)(2,1)} fusion(bf16[64,8,2048]{2,1,0:T(8,128)(2,1)} %bitcast.146, bf16[64,8,2048]{2,1,0:T(8,128)(2,1)} %bitcast.145), kind=kLoop, calls=%fused_computation.3 | loop fusion | flops 8388608 | bytes 8388608 | tf_op jit(solution)/shard_map/concatenate | solution.py:123
  331.8 12.4 %reduce-scatter.10.cloned.1.call-done = f32[96,16]{1,0:T(8,128)} async-done(((f32[384,16]{1,0:T(8,128)}), f32[96,16]{1,0:T(8,128)}) %reduce-scatter.10.cloned.1.call-update) | async-done | bytes 6160
  344.2 0.9 fusion.21
  345.3 2.2 fusion.3
  347.5 3.3 fusion.1
  (47 shorter events, 2.5 us)
Async XLA Ops:
  7.2 9.9 %copy-start = (bf16[128,8,1024]{2,1,0:T(8,128)(2,1)S(1)}, bf16[128,8,1024]{2,1,0:T(8,128)(2,1)}, u32[]{:S(2)}) copy-start(bf16[128,8,1024]{2,1,0:T(8,128)(2,1)} %param.14) | copy-start | bytes 6291460
  9.8 22.8 %all-to-all-start = ((bf16[8,64,512]{2,1,0:T(8,128)(2,1)}), bf16[8,64,512]{2,1,0:T(8,128)(2,1)}, u32[]{:S(2)}, u32[]{:S(2)}) async-start(bf16[8,64,512]{2,1,0:T(8,128)(2,1)} %broadcast_in_dim.24), calls=%async_computation | async-start | bytes 1048576 | tf_op jit(solution)/shard_map/all_to_all | solution.py:41
  17.5 1.0 copy-start.6
  32.6 33.6 %all-to-all-start.1 = ((bf16[4,128,1280]{2,1,0:T(8,128)(2,1)}), bf16[4,128,1280]{2,1,0:T(8,128)(2,1)S(1)}, u32[]{:S(2)}, u32[]{:S(2)}) async-start(bf16[4,128,1280]{2,1,0:T(8,128)(2,1)} %pad_maximum_fusion.1), calls=%async_computation.1 | async-start | bytes 2621440 | tf_op jit(solution)/shard_map/all_to_all | solution.py:31
  66.2 51.3 %all-to-all-start.2 = ((bf16[4,128,2048]{1,2,0:T(8,128)(2,1)}), bf16[4,128,2048]{1,2,0:T(8,128)(2,1)S(1)}, u32[]{:S(2)}, u32[]{:S(2)}) async-start(bf16[4,128,2048]{1,2,0:T(8,128)(2,1)} %bitcast.5), calls=%async_computation.2 | async-start | bytes 4194304 | tf_op jit(solution)/shard_map/all_to_all | solution.py:31
  69.8 150.7 %reduce-scatter.8.cloned.1.call-start = ((), (), s32[]{:S(2)}) async-start(), calls=%async_computation.11 | async-start | bytes 1966080 | tf_op jit(solution)/shard_map/reduce_scatter | solution.py:105
  74.0 3.3 copy-start.5
  120.1 141.6 %reduce-scatter.6.cloned.1.call-start = ((), (), s32[]{:S(2)}) async-start(), calls=%async_computation.10 | async-start | bytes 7864320 | tf_op jit(solution)/shard_map/reduce_scatter | solution.py:104
  120.8 51.3 %all-to-all-start.3 = ((bf16[4,128,2048]{1,2,0:T(8,128)(2,1)}), bf16[4,128,2048]{1,2,0:T(8,128)(2,1)S(1)}, u32[]{:S(2)}, u32[]{:S(2)}) async-start(bf16[4,128,2048]{1,2,0:T(8,128)(2,1)} %bitcast.2), calls=%async_computation.3 | async-start | bytes 4194304 | tf_op jit(solution)/shard_map/all_to_all | solution.py:31
  172.1 1.3 copy-start.4
  173.4 35.2 %all-to-all-start.4 = ((bf16[8,64,1280]{2,1,0:T(8,128)(2,1)}), bf16[8,64,1280]{2,1,0:T(8,128)(2,1)S(1)}, u32[]{:S(2)}, u32[]{:S(2)}) async-start(bf16[8,64,1280]{2,1,0:T(8,128)(2,1)} %bitcast.14), calls=%async_computation.4 | async-start | bytes 2621440 | tf_op jit(solution)/shard_map/all_to_all | solution.py:41
  177.0 89.6 %all-gather.3.cloned.1.call-start = ((), (), s32[]{:S(2)}) async-start(), calls=%async_computation.12 | async-start | bytes 6553600 | tf_op jit(solution)/shard_map/all_gather | solution.py:113
  208.7 1.1 copy-start.2
  209.8 4.7 %copy-start.3 = (bf16[8,64,1280]{2,1,0:T(8,128)(2,1)S(1)}, bf16[8,64,1280]{2,1,0:T(8,128)(2,1)}, u32[]{:S(2)}) copy-start(bf16[8,64,1280]{2,1,0:T(8,128)(2,1)} %copy-done.2) | copy-start | bytes 3932164
  209.8 51.9 %all-to-all-start.5 = ((bf16[8,64,2048]{2,1,0:T(8,128)(2,1)}), bf16[8,64,2048]{2,1,0:T(8,128)(2,1)}, u32[]{:S(2)}, u32[]{:S(2)}) async-start(bf16[8,64,2048]{2,1,0:T(8,128)(2,1)} %bitcast.156), calls=%async_computation.5 | async-start | bytes 4194304 | tf_op jit(solution)/shard_map/all_to_all | solution.py:41
  217.2 1.1 slice-start
  261.7 4.5 %copy-start.7 = (s32[64]{0:T(128)S(1)}, s32[64]{0:T(128)}, u32[]{:S(2)}) copy-start(s32[64]{0:T(128)} %param.10) | copy-start | bytes 772
  261.7 51.4 %all-to-all-start.6 = ((bf16[8,64,2048]{2,1,0:T(8,128)(2,1)}), bf16[8,64,2048]{2,1,0:T(8,128)(2,1)}, u32[]{:S(2)}, u32[]{:S(2)}) async-start(bf16[8,64,2048]{2,1,0:T(8,128)(2,1)} %bitcast.155), calls=%async_computation.8 | async-start | bytes 4194304 | tf_op jit(solution)/shard_map/all_to_all | solution.py:41
  266.2 78.0 %reduce-scatter.10.cloned.1.call-start = ((), (), s32[]{:S(2)}) async-start(), calls=%async_computation.13 | async-start | bytes 245760
  345.2 5.5 %copy-start.1 = (bf16[128,8,1024]{2,1,0:T(8,128)(2,1)S(1)}, bf16[128,8,1024]{2,1,0:T(8,128)(2,1)}, u32[]{:S(2)}) copy-start(bf16[128,8,1024]{2,1,0:T(8,128)(2,1)} %param.14) | copy-start | bytes 6291460
Sparse Core Ops, SparseCore 0:
  120.2 26.2 reduce-scatter.7
  149.2 58.3 reduce-scatter.5
  209.9 39.6 all-gather.2
  327.1 17.0 reduce-scatter.9

commit v4 on v3

--- a/solution.py
+++ b/solution.py
@@ -1,6 +1,8 @@
 import jax
 import jax.numpy as jnp
 from jax import lax
+from jax.experimental import pallas as pl
+from jax.experimental.pallas import tpu as pltpu
 from jax.sharding import PartitionSpec as P
 
 ADAPTER_SCALE = 2.0
@@ -54,6 +56,45 @@
         .transpose(1, 2, 0, 3)
         .reshape(tasks, ranks, -1)
     )
+
+
+def project_kernel(tokens_ref, factors_ref, mask_ref, pick_ref, out_ref):
+    owners, _, flat = factors_ref.shape
+    own = tokens_ref.shape[1] // owners
+    total = None
+    for owner in range(owners):
+        stacked = jnp.concatenate(
+            [factors_ref[owner, :, at : at + own] for at in range(0, flat, own)], axis=0
+        )
+        made = lax.dot_general(
+            tokens_ref[:, owner * own : (owner + 1) * own],
+            stacked,
+            (((1,), (1,)), ((), ())),
+            preferred_element_type=jnp.float32,
+        )
+        total = made if total is None else total + made
+    out_ref[...] = jnp.dot(
+        total * mask_ref[...],
+        pick_ref[...],
+        precision=lax.Precision.HIGHEST,
+        preferred_element_type=jnp.float32,
+    )
+
+
+def project_flat(tokens, got, mask, pick):
+    rows, width = tokens.shape
+    return pl.pallas_call(
+        project_kernel,
+        out_shape=jax.ShapeDtypeStruct((rows, pick.shape[1]), jnp.float32),
+        in_specs=[pl.BlockSpec(memory_space=pltpu.VMEM)] * 4,
+        out_specs=pl.BlockSpec(memory_space=pltpu.VMEM),
+        compiler_params=pltpu.CompilerParams(vmem_limit_bytes=24 * 2**20),
+        cost_estimate=pl.CostEstimate(
+            flops=2 * rows * width * mask.shape[1],
+            bytes_accessed=2 * (tokens.size + got.size) + 4 * mask.size,
+            transcendentals=0,
+        ),
+    )(tokens, got, mask, pick)
 
 
 def local(
@@ -134,8 +175,19 @@
         )
         return jnp.sum(made * member[..., None], axis=2).reshape(rows, rank)
 
+    if (shard_width // n_owners) % 128 == 0:
+        tasks = task_counts.shape[0]
+        same = jnp.repeat(jnp.eye(blocks, dtype=jnp.float32), block_tasks, axis=1)
+        mask = jnp.tile(member, (1, 1, blocks)) * same[:, None, :]
+        mask = jnp.tile(mask.reshape(rows, tasks), (1, rank))
+        pick = jnp.repeat(jnp.eye(2 * rank, dtype=jnp.float32), tasks, axis=0)
+        sums = project_flat(tokens, got0, mask, pick[: rank * tasks]) + project_flat(
+            tokens, got1, mask, pick[rank * tasks :]
+        )
+    else:
+        sums = jnp.concatenate((project(half0), project(half1)), axis=1)
     low_rank = lax.psum_scatter(
-        jnp.concatenate((project(half0), project(half1)), axis=1),
+        sums,
         "tensor", scatter_dimension=0, tiled=True,
     )
     own_member = lax.dynamic_index_in_dim(

time: 359 us -> 353 us (0.983)
  Pallas kernels: 0 us -> 6.65 us
  matrix products: 40.9 us -> 36.4 us
  local copies, waits for them, and re-layouts: 67.9 us -> 64 us
    unnamed x5 -> x4, waiting for transfers between devices: 13.2 us -> 0.74 us
    reduce_scatter x0 -> x1, waiting for transfers between devices: none -> 10.5 us  [local(): low_rank = lax.psum_scatter(sums, 'tensor', scatter_dimension=0, tiled=True)]
    pallas_call x0 -> x2, Pallas kernels: none -> 6.65 us  [project_flat(): pl.pallas_call(project_kernel, out_shape=jax.ShapeDtypeStruct((rows, pick...]
    transpose x3 -> x5, local copies, waits for them, and re-layouts: 7.98 us -> 2.19 us  [unpack_factor(): return got.reshape(owners, tasks, ranks, flat // ranks).transpose(1, 2, 0...]
    dot_general x2 -> x0, matrix products: 4.23 us -> none  [project(): jnp.einsum('bpd,bmrd->bpmr', stretches, half.reshape(blocks, block_tasks,...]
    unnamed x29 -> x36, local copies, waits for them, and re-layouts: 19.8 us -> 18.7 us
  transfers between devices with their start and end apart: 11 -> 11, of which waited for: 8 -> 8; matrix products, arithmetic and copies ran while one was open for 24% -> 24% of each run, Pallas kernels for 0% -> 1%
where the time goes in v4:
time: 353 us; the launch traced here: 352 us
  waiting for transfers between devices  194 us (55%)
  local copies, waits for them, and re-layouts  64 us (18%)
  matrix products  36.4 us (10%)
  starting transfers between devices  31.3 us (9%)
  between operations  14.2 us (4%)
  Pallas kernels  6.65 us (2%)
  other arithmetic  4.7 us (1%)
    all_to_all x4, waiting for transfers between devices, to_owners(): lax.all_to_all(made, ('groups', 'task'), split_axis=0, concat_axis=0, til...  100 us
    all_to_all x3, waiting for transfers between devices, regroup(): lax.all_to_all(packed, 'task', split_axis=0, concat_axis=0, tiled=True)  83.2 us
    all_to_all x4, starting transfers between devices, to_owners(): lax.all_to_all(made, ('groups', 'task'), split_axis=0, concat_axis=0, til...  19.2 us
    unnamed x36, local copies, waits for them, and re-layouts  18.7 us
    dot_general x3, matrix products, produce(): made = jnp.dot(every_hidden, matrix, preferred_element_type=jnp.float32)  12.1 us
    dot_general x1, matrix products, local(): sums_query = jnp.dot(tokens, w_query, preferred_element_type=jnp.float32)  11.9 us
    all_to_all x3, starting transfers between devices, regroup(): lax.all_to_all(packed, 'task', split_axis=0, concat_axis=0, tiled=True)  11.8 us
    reduce_scatter x1, waiting for transfers between devices, local(): low_rank = lax.psum_scatter(sums, 'tensor', scatter_dimension=0, tiled=True)  10.5 us
  transfers between devices with their start and end apart: 11, of which 8 were waited for; matrix products, arithmetic and copies ran while one was open for 24% of the time, Pallas kernels for 1%

profile of v4, /device:TPU:0, one launch (start us, length us, event | category | flops | bytes accessed | tf_op | source)
XLA Modules:
  0.0 351.7 jit_solution(1074071707893601062)
XLA Ops:
  7.2 1.8 multiply_convert_fusion
  9.0 0.8 broadcast_in_dim.43
  9.8 7.3 %all-to-all-start = ((bf16[8,64,512]{2,1,0:T(8,128)(2,1)}), bf16[8,64,512]{2,1,0:T(8,128)(2,1)}, u32[]{:S(2)}, u32[]{:S(2)}) async-start(bf16[8,64,512]{2,1,0:T(8,128)(2,1)} %broadcast_in_dim.43), calls=%async_computation | async-start | bytes 1048576 | tf_op jit(solution)/shard_map/all_to_all | solution.py:43
  17.7 0.3 reshape.183
  18.0 0.3 copy.109
  18.3 1.2 pad_maximum_fusion.1
  19.5 13.1 %all-to-all-done = bf16[8,64,512]{2,1,0:T(8,128)(2,1)} async-done(((bf16[8,64,512]{2,1,0:T(8,128)(2,1)}), bf16[8,64,512]{2,1,0:T(8,128)(2,1)}, u32[]{:S(2)}, u32[]{:S(2)}) %all-to-all-start) | async-done | bytes 524320 | tf_op jit(solution)/shard_map/all_to_all | solution.py:43
  32.6 3.5 %all-to-all-start.1 = ((bf16[4,128,1280]{2,1,0:T(8,128)(2,1)}), bf16[4,128,1280]{2,1,0:T(8,128)(2,1)S(1)}, u32[]{:S(2)}, u32[]{:S(2)}) async-start(bf16[4,128,1280]{2,1,0:T(8,128)(2,1)} %pad_maximum_fusion.1), calls=%async_computation.1 | async-start | bytes 2621440 | tf_op jit(solution)/shard_map/all_to_all | solution.py:33
  36.1 4.0 %fusion.18 = (bf16[128,8,2048]{2,1,0:T(8,128)(2,1)S(1)}, bf16[128,8,2048]{2,1,0:T(8,128)(2,1)S(1)}) fusion(bf16[128,16,2048]{2,1,0:T(8,128)(2,1)} %param.13), kind=kLoop, calls=%fused_computation.45 | loop fusion | bytes 16777216 | tf_op jit(solution)/shard_map/slice | solution.py:134
  40.1 2.5 constant_dynamic-slice_fusion.4
  42.7 3.3 copy.130
  46.0 1.5 copy.106
  47.5 18.7 %all-to-all-done.1 = bf16[4,128,1280]{2,1,0:T(8,128)(2,1)S(1)} async-done(((bf16[4,128,1280]{2,1,0:T(8,128)(2,1)}), bf16[4,128,1280]{2,1,0:T(8,128)(2,1)S(1)}, u32[]{:S(2)}, u32[]{:S(2)}) %all-to-all-start.1) | async-done | bytes 1310752 | tf_op jit(solution)/shard_map/all_to_all | solution.py:33
  66.2 4.6 %all-to-all-start.2 = ((bf16[4,128,2048]{1,2,0:T(8,128)(2,1)}), bf16[4,128,2048]{1,2,0:T(8,128)(2,1)}, u32[]{:S(2)}, u32[]{:S(2)}) async-start(bf16[4,128,2048]{1,2,0:T(8,128)(2,1)} %bitcast.5), calls=%async_computation.2 | async-start | bytes 4194304 | tf_op jit(solution)/shard_map/all_to_all | solution.py:33
  70.9 2.9 copy.128
  73.8 3.3 copy.104
  77.1 5.2 %fusion.22 = f32[384,1024]{1,0:T(8,128)} fusion(bf16[384,2048]{1,0:T(8,128)(2,1)S(1)} %copy-done.2, bf16[2048,1024]{1,0:T(8,128)(2,1)} %param.17), kind=kOutput, calls=%fused_computation.49 | convolution fusion | flops 1610612736 | bytes 7340032 | tf_op jit(solution)/shard_map/dot_general | solution.py:139
  82.3 11.9 %fusion.21 = f32[384,4096]{1,0:T(8,128)} fusion(bf16[384,2048]{1,0:T(8,128)(2,1)S(1)} %copy-done.2, bf16[2048,4096]{1,0:T(8,128)(2,1)} %param.16), kind=kOutput, calls=%fused_computation.48 | convolution fusion | flops 6442450944 | bytes 24641536 | tf_op jit(solution)/shard_map/dot_general | solution.py:138
  94.2 3.0 convolution_convert_fusion.2
  97.2 21.5 %all-to-all-done.2 = bf16[4,128,2048]{1,2,0:T(8,128)(2,1)} async-done(((bf16[4,128,2048]{1,2,0:T(8,128)(2,1)}), bf16[4,128,2048]{1,2,0:T(8,128)(2,1)}, u32[]{:S(2)}, u32[]{:S(2)}) %all-to-all-start.2) | async-done | bytes 2097184 | tf_op jit(solution)/shard_map/all_to_all | solution.py:33
  118.6 3.9 %copy.111 = bf16[4,128,2048]{2,1,0:T(8,128)(2,1)} copy(bf16[4,128,2048]{1,2,0:T(8,128)(2,1)} %all-to-all-done.2) | data formatting | bytes 4194304 | tf_op jit(solution)/shard_map/all_to_all | solution.py:33
  122.6 0.7 reduce-scatter.4.cloned.1.call-update
  123.3 3.7 %all-to-all-start.3 = ((bf16[4,128,2048]{1,2,0:T(8,128)(2,1)}), bf16[4,128,2048]{1,2,0:T(8,128)(2,1)S(1)}, u32[]{:S(2)}, u32[]{:S(2)}) async-start(bf16[4,128,2048]{1,2,0:T(8,128)(2,1)} %bitcast.2), calls=%async_computation.3 | async-start | bytes 4194304 | tf_op jit(solution)/shard_map/all_to_all | solution.py:33
  127.0 4.6 %convolution_convert_fusion.1 = bf16[512,2048]{1,0:T(8,128)(2,1)} fusion(bf16[512,512]{1,0:T(8,128)(2,1)} %bitcast.6, bf16[512,2048]{1,0:T(8,128)(2,1)} %bitcast.130), kind=kOutput, calls=%fused_computation.5 | convolution fusion | flops 1074790400 | bytes 4718592 | tf_op jit(solution)/shard_map/dot_general | solution.py:38
  131.6 43.0 %all-to-all-done.3 = bf16[4,128,2048]{1,2,0:T(8,128)(2,1)S(1)} async-done(((bf16[4,128,2048]{1,2,0:T(8,128)(2,1)}), bf16[4,128,2048]{1,2,0:T(8,128)(2,1)S(1)}, u32[]{:S(2)}, u32[]{:S(2)}) %all-to-all-start.3) | async-done | bytes 2097184 | tf_op jit(solution)/shard_map/all_to_all | solution.py:33
  174.6 1.3 copy-done.7
  175.9 3.6 %all-to-all-start.4 = ((bf16[8,64,1280]{2,1,0:T(8,128)(2,1)}), bf16[8,64,1280]{2,1,0:T(8,128)(2,1)S(1)}, u32[]{:S(2)}, u32[]{:S(2)}) async-start(bf16[8,64,1280]{2,1,0:T(8,128)(2,1)} %bitcast.14), calls=%async_computation.4 | async-start | bytes 2621440 | tf_op jit(solution)/shard_map/all_to_all | solution.py:43
  179.6 4.1 %copy.112 = bf16[4,128,2048]{2,1,0:T(8,128)(2,1)} copy(bf16[4,128,2048]{1,2,0:T(8,128)(2,1)} %copy-done.7) | data formatting | bytes 4194304 | tf_op jit(solution)/shard_map/all_to_all | solution.py:33
  183.6 4.5 %convolution_convert_fusion = bf16[512,2048]{1,0:T(8,128)(2,1)} fusion(bf16[512,512]{1,0:T(8,128)(2,1)} %bitcast.6, bf16[512,2048]{1,0:T(8,128)(2,1)} %bitcast.131), kind=kOutput, calls=%fused_computation.4 | convolution fusion | flops 1074790400 | bytes 4718592 | tf_op jit(solution)/shard_map/dot_general | solution.py:38
  188.1 23.0 %all-to-all-done.4 = bf16[8,64,1280]{2,1,0:T(8,128)(2,1)S(1)} async-done(((bf16[8,64,1280]{2,1,0:T(8,128)(2,1)}), bf16[8,64,1280]{2,1,0:T(8,128)(2,1)S(1)}, u32[]{:S(2)}, u32[]{:S(2)}) %all-to-all-start.4) | async-done | bytes 1310752 | tf_op jit(solution)/shard_map/all_to_all | solution.py:43
  211.2 1.1 copy-done.5
  212.3 3.9 %all-to-all-start.5 = ((bf16[8,64,2048]{2,1,0:T(8,128)(2,1)}), bf16[8,64,2048]{2,1,0:T(8,128)(2,1)S(1)}, u32[]{:S(2)}, u32[]{:S(2)}) async-start(bf16[8,64,2048]{2,1,0:T(8,128)(2,1)} %bitcast.129), calls=%async_computation.5 | async-start | bytes 4194304 | tf_op jit(solution)/shard_map/all_to_all | solution.py:43
  216.2 1.1 slice.42
  217.3 2.7 copy.114
  220.0 1.6 copy.132
  221.7 1.1 copy_bitcast_fusion.1
  222.8 40.9 %all-to-all-done.5.factors_ref = bf16[8,64,2048]{2,1,0:T(8,128)(2,1)S(1)} async-done(((bf16[8,64,2048]{2,1,0:T(8,128)(2,1)}), bf16[8,64,2048]{2,1,0:T(8,128)(2,1)S(1)}, u32[]{:S(2)}, u32[]{:S(2)}) %all-to-all-start.5) | async-done | bytes 2097184 | tf_op jit(solution)/shard_map/all_to_all | solution.py:43
  263.7 4.5 %all-to-all-start.6 = ((bf16[8,64,2048]{2,1,0:T(8,128)(2,1)}), bf16[8,64,2048]{2,1,0:T(8,128)(2,1)}, u32[]{:S(2)}, u32[]{:S(2)}) async-start(bf16[8,64,2048]{2,1,0:T(8,128)(2,1)} %bitcast.128), calls=%async_computation.8 | async-start | bytes 4194304 | tf_op jit(solution)/shard_map/all_to_all | solution.py:43
  269.2 0.9 tile.19
  270.2 1.4 copy.118.mask_ref
  271.7 1.3 constant_dynamic-slice_fusion
  273.0 0.3 copy.133
  273.4 1.7 copy.143
  275.0 1.7 constant_dynamic-slice_fusion.1
  276.7 2.4 reshape.198
  279.1 2.9 copy.123
  282.0 2.9 reshape.199
  284.9 0.7 copy.135
  285.8 1.6 copy.124
  287.4 1.0 copy.126
  288.4 1.4 copy-done.3
  289.8 2.5 shard_map.128
  292.3 22.9 %all-to-all-done.6.factors_ref = bf16[8,64,2048]{2,1,0:T(8,128)(2,1)} async-done(((bf16[8,64,2048]{2,1,0:T(8,128)(2,1)}), bf16[8,64,2048]{2,1,0:T(8,128)(2,1)}, u32[]{:S(2)}, u32[]{:S(2)}) %all-to-all-start.6) | async-done | bytes 2097184 | tf_op jit(solution)/shard_map/all_to_all | solution.py:43
  315.2 1.4 copy-done.4
  316.6 4.1 %shard_map.129 = f32[384,16]{1,0:T(8,128)S(1)} custom-call(bf16[384,2048]{1,0:T(8,128)(2,1)S(1)} %copy-done.4, bf16[8,64,2048]{2,1,0:T(8,128)(2,1)} %all-to-all-done.6.factors_ref, f32[384,512]{1,0:T(8,128)S(1)} %copy.118.mask_ref, f32[512,16]{1,0:T(8,128)S(1)} %bitcast.114), custom_call_target="tpu_custom_call" | custom-call | flops 805306368 | bytes 4456448 | tf_op jit(solution)/shard_map/pallas_call | solution.py:86
  320.7 0.7 add.41
  321.4 2.3 copy.136
  323.9 0.3 copy.125
  324.2 1.3 copy-done.8
  325.5 2.5 pad_maximum_fusion
  328.0 10.5 %reduce-scatter.8.cloned.1.call-done = f32[96,16]{1,0:T(8,128)} async-done(((f32[384,16]{1,0:T(8,128)}), f32[96,16]{1,0:T(8,128)}) %reduce-scatter.8.cloned.1.call-update) | async-done | bytes 6160 | tf_op jit(solution)/shard_map/reduce_scatter | solution.py:189
  338.6 0.9 fusion.19
  339.7 3.4 fusion.1
  343.1 2.0 fusion.3
  (65 shorter events, 2.4 us)
Async XLA Ops:
  7.2 10.4 %copy-start = (bf16[128,8,1024]{2,1,0:T(8,128)(2,1)S(1)}, bf16[128,8,1024]{2,1,0:T(8,128)(2,1)}, u32[]{:S(2)}) copy-start(bf16[128,8,1024]{2,1,0:T(8,128)(2,1)} %param.14) | copy-start | bytes 6291460
  7.2 9.9 %copy-start.12 = (bf16[128,8,256]{2,1,0:T(8,128)(2,1)S(1)}, bf16[128,8,256]{2,1,0:T(8,128)(2,1)}, u32[]{:S(2)}) copy-start(bf16[128,8,256]{2,1,0:T(8,128)(2,1)} %param.15) | copy-start | bytes 1572868
  9.8 22.8 %all-to-all-start = ((bf16[8,64,512]{2,1,0:T(8,128)(2,1)}), bf16[8,64,512]{2,1,0:T(8,128)(2,1)}, u32[]{:S(2)}, u32[]{:S(2)}) async-start(bf16[8,64,512]{2,1,0:T(8,128)(2,1)} %broadcast_in_dim.43), calls=%async_computation | async-start | bytes 1048576 | tf_op jit(solution)/shard_map/all_to_all | solution.py:43
  32.6 33.6 %all-to-all-start.1 = ((bf16[4,128,1280]{2,1,0:T(8,128)(2,1)}), bf16[4,128,1280]{2,1,0:T(8,128)(2,1)S(1)}, u32[]{:S(2)}, u32[]{:S(2)}) async-start(bf16[4,128,1280]{2,1,0:T(8,128)(2,1)} %pad_maximum_fusion.1), calls=%async_computation.1 | async-start | bytes 2621440 | tf_op jit(solution)/shard_map/all_to_all | solution.py:33
  66.2 4.7 %copy-start.9 = (bf16[128,8,1024]{2,1,0:T(8,128)(2,1)S(1)}, bf16[128,8,1024]{2,1,0:T(8,128)(2,1)}, u32[]{:S(2)}) copy-start(bf16[128,8,1024]{2,1,0:T(8,128)(2,1)} %get-tuple-element.75) | copy-start | bytes 6291460
  66.2 52.4 %all-to-all-start.2 = ((bf16[4,128,2048]{1,2,0:T(8,128)(2,1)}), bf16[4,128,2048]{1,2,0:T(8,128)(2,1)}, u32[]{:S(2)}, u32[]{:S(2)}) async-start(bf16[4,128,2048]{1,2,0:T(8,128)(2,1)} %bitcast.5), calls=%async_computation.2 | async-start | bytes 4194304 | tf_op jit(solution)/shard_map/all_to_all | solution.py:33
  70.9 151.9 %reduce-scatter.6.cloned.1.call-start = ((), (), s32[]{:S(2)}) async-start(), calls=%async_computation.11 | async-start | bytes 1966080 | tf_op jit(solution)/shard_map/reduce_scatter | solution.py:146
  73.8 3.3 copy-start.2
  122.6 141.1 %reduce-scatter.4.cloned.1.call-start = ((), (), s32[]{:S(2)}) async-start(), calls=%async_computation.10 | async-start | bytes 7864320 | tf_op jit(solution)/shard_map/reduce_scatter | solution.py:145
  123.3 51.3 %all-to-all-start.3 = ((bf16[4,128,2048]{1,2,0:T(8,128)(2,1)}), bf16[4,128,2048]{1,2,0:T(8,128)(2,1)S(1)}, u32[]{:S(2)}, u32[]{:S(2)}) async-start(bf16[4,128,2048]{1,2,0:T(8,128)(2,1)} %bitcast.2), calls=%async_computation.3 | async-start | bytes 4194304 | tf_op jit(solution)/shard_map/all_to_all | solution.py:33
  174.6 1.3 copy-start.7
  175.9 35.2 %all-to-all-start.4 = ((bf16[8,64,1280]{2,1,0:T(8,128)(2,1)}), bf16[8,64,1280]{2,1,0:T(8,128)(2,1)S(1)}, u32[]{:S(2)}, u32[]{:S(2)}) async-start(bf16[8,64,1280]{2,1,0:T(8,128)(2,1)} %bitcast.14), calls=%async_computation.4 | async-start | bytes 2621440 | tf_op jit(solution)/shard_map/all_to_all | solution.py:43
  179.5 92.1 %all-gather.3.cloned.1.call-start = ((), (), s32[]{:S(2)}) async-start(), calls=%async_computation.13 | async-start | bytes 6553600 | tf_op jit(solution)/shard_map/all_gather | solution.py:154
  211.2 1.1 copy-start.5
  212.3 3.9 %copy-start.6 = (bf16[8,64,1280]{2,1,0:T(8,128)(2,1)S(1)}, bf16[8,64,1280]{2,1,0:T(8,128)(2,1)}, u32[]{:S(2)}) copy-start(bf16[8,64,1280]{2,1,0:T(8,128)(2,1)} %copy-done.5) | copy-start | bytes 3932164
  212.3 51.4 %all-to-all-start.5 = ((bf16[8,64,2048]{2,1,0:T(8,128)(2,1)}), bf16[8,64,2048]{2,1,0:T(8,128)(2,1)S(1)}, u32[]{:S(2)}, u32[]{:S(2)}) async-start(bf16[8,64,2048]{2,1,0:T(8,128)(2,1)} %bitcast.129), calls=%async_computation.5 | async-start | bytes 4194304 | tf_op jit(solution)/shard_map/all_to_all | solution.py:43
  220.0 1.6 slice-start
  263.7 4.5 %copy-start.13 = (s32[64]{0:T(128)S(1)}, s32[64]{0:T(128)}, u32[]{:S(2)}) copy-start(s32[64]{0:T(128)} %param.10) | copy-start | bytes 772
  263.7 51.4 %all-to-all-start.6 = ((bf16[8,64,2048]{2,1,0:T(8,128)(2,1)}), bf16[8,64,2048]{2,1,0:T(8,128)(2,1)}, u32[]{:S(2)}, u32[]{:S(2)}) async-start(bf16[8,64,2048]{2,1,0:T(8,128)(2,1)} %bitcast.128), calls=%async_computation.8 | async-start | bytes 4194304 | tf_op jit(solution)/shard_map/all_to_all | solution.py:43
  268.2 70.4 %reduce-scatter.8.cloned.1.call-start = ((), (), s32[]{:S(2)}) async-start(), calls=%async_computation.12 | async-start | bytes 245760 | tf_op jit(solution)/shard_map/reduce_scatter | solution.py:189
  288.4 1.4 copy-start.3
  315.2 1.4 copy-start.4
  323.9 1.6 copy-start.8
  325.5 14.2 %copy-start.10 = (bf16[16,8,32,128]{3,2,1,0:T(8,128)(2,1)S(1)}, bf16[16,8,32,128]{3,2,1,0:T(8,128)(2,1)}, u32[]{:S(2)}) copy-start(bf16[16,8,32,128]{3,2,1,0:T(8,128)(2,1)} %copy.143) | copy-start | bytes 3145732
  328.0 15.1 %copy-start.11 = (bf16[128,1024]{1,0:T(8,128)(2,1)S(1)}, bf16[128,1024]{1,0:T(8,128)(2,1)}, u32[]{:S(2)}) copy-start(bf16[128,1024]{1,0:T(8,128)(2,1)} %reshape.199) | copy-start | bytes 786436
  339.6 5.5 %copy-start.1 = (bf16[128,8,1024]{2,1,0:T(8,128)(2,1)S(1)}, bf16[128,8,1024]{2,1,0:T(8,128)(2,1)}, u32[]{:S(2)}) copy-start(bf16[128,8,1024]{2,1,0:T(8,128)(2,1)} %param.14) | copy-start | bytes 6291460
Sparse Core Ops, SparseCore 0:
  122.7 26.2 reduce-scatter.5
  151.7 58.3 reduce-scatter.3
  212.4 39.7 all-gather.2
  321.6 16.9 reduce-scatter.7
